TPU v7x, 256 devices: a whole 4x4x8 slice. The times are simulated.
256 devices in a mesh: bead: 16 (over z_lo, y), space: 16 (over x, z_hi, core).
Axes of the slice: x: 4, y: 4, z: 8 (z_hi: 2, z_lo: 4; z = z_hi * 4 + z_lo), core: 2. Of those that a mesh axis runs over, the one named last changes fastest.
Arguments:
- positions: float32 [32, 3, 4096], P('bead', None, 'space'), may hold values from -6 to 6
- momenta: float32 [32, 3, 4096], P('bead', None, 'space'), may hold values from -12 to 12
- species: int32 [4096], P('space'), may hold values 0 or 1
- neighbours: int32 [128, 4096], P(None, 'space'), may hold values from 0 to 512, as said below
- ghost_index: int32 [2, 2048], P(None, 'space'), may hold values from 0 to 255, as said below
- sparse_points: float32 [64, 512], replicated, may hold values from -6 to 6
- coefficients: float32 [2, 512], replicated, may hold values from -6 to 6
- noise: float32 [32, 6, 4096], P('bead', None, 'space'), may hold values from -6 to 6
Outputs:
- new_positions: float32 [32, 3, 4096], P('bead', None, 'space')
- new_momenta: float32 [32, 3, 4096], P('bead', None, 'space')
- forces: float32 [32, 3, 4096], P('bead', None, 'space')
Inputs may be any that keep to these rules, and one draw needn't show every extreme that they name: A column lists an atom's neighbours as indices into its slab's table: 0 to 255 own atoms, then 128 atoms from the slab below, then 128 from the slab above; 512 marks padding, which follows the real entries. An atom never lists itself. An atom in its slab's lower face list references only own atoms and atoms from below, one in the upper face list only own atoms and atoms from above. Every atom has 64 or more real entries, and some atom of every slab has 128. `ghost_index`: columns s * 128 to (s + 1) * 128 - 1 belong to slab s and hold indices of its own atoms, 0 to 255; the two rows of a slab together name each of its atoms once.
All inputs are finite; a program needn't handle non-finite values. No bound on the sum of `species` on one device may be relied on, other than what follows from the above.
Results may differ from a plain program's by a relative error of at most 0.0003.
Values sent between devices are 32-bit elements; how exact they have to be, the bound alone decides.
No kernel may reach another device: no remote copies, remote signals or barrier semaphores. Data moves between devices by JAX's collectives and lax.ppermute only.
A program may use at most 64 MiB of HBM per device.

v0:
```python
import math

import jax
import jax.numpy as jnp
from jax import lax
from jax.sharding import PartitionSpec as P

BEADS = 32


cutoff = 5.0
soften = 0.25
time_step = 0.5
kick = 0.25
friction = 0.2
epsilon = 1e-06
oxygen_mass = 16.0
hydrogen_mass = 1.0


def extended(value, sides, width):
    for axis, dim in sides:
        size, length = (lax.axis_size(axis), value.shape[dim])
        up = [(i, (i + 1) % size) for i in range(size)]
        down = [(j, i) for i, j in up]
        last = lax.slice_in_dim(value, length - width, length, axis=dim)
        first = lax.slice_in_dim(value, 0, width, axis=dim)
        before = lax.ppermute(last, axis, up)
        after = lax.ppermute(first, axis, down)
        value = jnp.concatenate([before, value, after], axis=dim)
    return value


def normalize_columns(matrix):
    return matrix / jnp.sqrt(jnp.sum(matrix * matrix, axis=-2, keepdims=True) + epsilon)


def table_gradient(place, spec_table, neighbours, basis, coefficients):
    slots = neighbours.shape[0]
    size = neighbours.shape[1]
    width = place.shape[2] - 1
    block = math.gcd(size, max(8, 4096 // slots))
    nrad = basis.shape[0] // 2
    centers = cutoff * jnp.arange(nrad, dtype=jnp.float32) / nrad
    sharp = nrad * nrad / (2.0 * cutoff * cutoff)
    entries = jnp.arange(width + 1, dtype=jnp.int32)

    def advance(total, start):
        links = lax.dynamic_slice_in_dim(neighbours, start, block, 1)
        live = (links < width).astype(jnp.float32)
        safe = jnp.minimum(links, width)
        hydro = spec_table[safe]
        kind = lax.dynamic_slice_in_dim(spec_table, start, block, 0)
        weight = (
            coefficients[0][:, None] * (1.0 - kind)[None] + coefficients[1][:, None] * kind[None]
        )
        near = jnp.take(place, safe, axis=2)
        own = lax.dynamic_slice_in_dim(place, start, block, 2)

        def energy(near_pos, own_pos):
            delta = near_pos - own_pos[:, :, None, :]
            dist = jnp.sqrt(jnp.sum(delta * delta, axis=1) + soften)
            ratio = dist * dist / (cutoff * cutoff)
            smooth = jnp.where(dist < cutoff, (1.0 - ratio) ** 2, 0.0) * live[None]
            radial = (
                jnp.exp(-sharp * (dist[:, None] - centers[None, :, None, None]) ** 2)
                * smooth[:, None]
            )
            part_o = jnp.sum(radial * (1.0 - hydro)[None, None], axis=2)
            part_h = jnp.sum(radial * hydro[None, None], axis=2)
            unit = normalize_columns(jnp.concatenate([part_o, part_h], axis=1))
            intersection = jnp.einsum("dm,lda->lma", basis, unit, precision=lax.Precision.HIGHEST)
            return jnp.sum(weight[None] * intersection * intersection)

        grad_near, grad_own = jax.grad(energy, argnums=(0, 1))(near, own)
        select = (safe.reshape(-1)[:, None] == entries[None, :]).astype(jnp.float32)
        rows = grad_near.shape[0] * grad_near.shape[1]
        spread = jnp.dot(
            grad_near.reshape(rows, -1),
            select,
            precision=lax.Precision.HIGHEST,
            preferred_element_type=jnp.float32,
        )
        total = total + spread.reshape(total.shape)
        current = lax.dynamic_slice_in_dim(total, start, block, 2)
        total = lax.dynamic_update_slice_in_dim(total, current + grad_own, start, 2)
        return (total, None)

    starts = jnp.arange(size // block, dtype=jnp.int32) * block
    total, _ = lax.scan(advance, jnp.zeros_like(place), starts)
    return total


def mode_tables(count):
    index = jnp.arange(count, dtype=jnp.int32)
    phase = (index[:, None] * index[None, :] % count).astype(jnp.float32) * (2.0 * math.pi / count)
    column = index[None, :]
    scale = math.sqrt(2.0 / count)
    flat = 1.0 / math.sqrt(count)
    cmat = jnp.where(
        column == 0,
        flat,
        jnp.where(
            2 * column < count,
            scale * jnp.cos(phase),
            jnp.where(2 * column == count, flat * jnp.cos(phase), scale * jnp.sin(phase)),
        ),
    )
    freq = 2.0 * jnp.sin(index.astype(jnp.float32) * (math.pi / count))
    damping = jnp.where(index == 0, friction, 2.0 * freq)
    return (cmat, freq, damping)


def evolve(modes, noise, freq, damping, mass):
    freq = freq[:, None, None]
    keep = jnp.exp(-kick * damping)[:, None, None]
    fresh = jnp.sqrt(1.0 - keep * keep)
    weight = mass[None, None, :]
    amplitude = jnp.sqrt(weight)
    place = modes[:, 0:3]
    moment = keep * modes[:, 3:6] + fresh * amplitude * noise[:, 0:3]
    cosine = jnp.cos(time_step * freq)
    sine = jnp.sin(time_step * freq)
    spread = jnp.where(freq > 0, sine / jnp.where(freq > 0, freq, 1.0), time_step)
    place_new = cosine * place + spread * moment / weight
    moment = cosine * moment - weight * freq * sine * place
    moment = keep * moment + fresh * amplitude * noise[:, 3:6]
    return jnp.concatenate([place_new, moment], axis=1)


def per_device(
    positions, momenta, species, neighbours, ghost_index, sparse_points, coefficients, noise
):
    local_beads = positions.shape[0]
    atoms = positions.shape[2]
    ghosts = ghost_index.shape[1]
    kind = species.astype(jnp.float32)
    carried = jnp.concatenate(
        [positions, jnp.broadcast_to(kind[None, None, :], (local_beads, 1, atoms))], axis=1
    )
    faces = jnp.stack([carried[:, :, ghost_index[0]], carried[:, :, ghost_index[1]]])
    rims = extended(faces, (("space", 0),), 1)
    tables = jnp.concatenate(
        [carried, rims[0], rims[3], jnp.zeros((local_beads, 4, 1), jnp.float32)], axis=2
    )
    basis = normalize_columns(sparse_points)
    grads = table_gradient(tables[:, 0:3], tables[0, 3], neighbours, basis, coefficients)
    copies = jnp.stack(
        [grads[:, :, atoms : atoms + ghosts], grads[:, :, atoms + ghosts : atoms + 2 * ghosts]]
    )
    returned = extended(copies, (("space", 0),), 1)
    own = (
        grads[:, :, :atoms]
        .at[:, :, ghost_index[0]]
        .add(returned[0])
        .at[:, :, ghost_index[1]]
        .add(returned[3])
    )
    forces = -own
    half = momenta + kick * forces
    state = jnp.concatenate([positions, half], axis=1)
    cmat, freq, damping = mode_tables(BEADS)
    masses = jnp.where(species > 0, hydrogen_mass, oxygen_mass).astype(jnp.float32)
    columns, shaken = (
        lax.all_to_all(state, "bead", split_axis=2, concat_axis=0, tiled=True),
        lax.all_to_all(noise, "bead", split_axis=2, concat_axis=0, tiled=True),
    )
    piece = columns.shape[2]
    piece_mass = lax.dynamic_slice_in_dim(masses, lax.axis_index("bead") * piece, piece, 0)
    modes = jnp.einsum("bk,bra->kra", cmat, columns, precision=lax.Precision.HIGHEST)
    moved = evolve(modes, shaken, freq, damping, piece_mass)
    beads_all = jnp.einsum("bk,kra->bra", cmat, moved, precision=lax.Precision.HIGHEST)
    result = lax.all_to_all(beads_all, "bead", split_axis=0, concat_axis=2, tiled=True)
    return (result[:, 0:3], result[:, 3:6], forces)


def solution(mesh):
    placed = (
        P("bead", None, "space"),
        P("bead", None, "space"),
        P("space"),
        P(None, "space"),
        P(None, "space"),
        P(),
        P(),
        P("bead", None, "space"),
    )
    return jax.shard_map(
        per_device,
        mesh=mesh,
        in_specs=placed,
        out_specs=(P("bead", None, "space"), P("bead", None, "space"), P("bead", None, "space")),
        check_vma=False,
    )
```

profile of v0, /device:TPU:8, one launch (start us, length us, event | category | flops | bytes accessed | tf_op | source)
XLA Modules:
  0.0 603.8 jit_solution(241483960581493098)
XLA Ops:
  0.6 0.8 fusion.53
  2.1 0.9 copy.183
  3.6 0.7 gather_fusion.2
  5.2 8.9 %collective-permute-start.1 = (f32[1,2,4,128]{2,1,3,0:T(2,128)S(1)}, f32[1,2,4,128]{2,1,3,0:T(2,128)S(1)}, u32[]{:S(2)}, u32[]{:S(2)}) collective-permute-start(f32[1,2,4,128]{2,1,3,0:T(2,128)S(1)} %bitcast.134), channel_id=1, source_target_pairs={{1,0},{2,1},{3,2},{4,3},{5,4},{6,5},{7,6},{8,7},{9,8},{10,9},{11,1... | collective-permute-start | bytes 12296 | tf_op jit(solution)/shard_map/ppermute | solution.py:29
  14.1 0.9 copy.195
  15.0 1.0 reshape.409
  16.0 7.9 %all-to-all-start.1 = ((f32[16,1,192]{2,1,0:T(1,128)}), f32[16,1,192]{2,1,0:T(1,128)S(1)}, u32[]{:S(2)}, u32[]{:S(2)}) async-start(f32[16,1,192]{2,1,0:T(1,128)} %reshape.409), calls=%async_computation.1 | async-start | bytes 32768 | tf_op jit(solution)/shard_map/all_to_all | solution.py:166
  24.9 0.9 multiply_reduce_fusion.3
  25.8 0.9 broadcast_divide_fusion
  27.6 524.9 %while.11 = (s32[]{:T(128)}, f32[2,3,513]{2,0,1:T(2,128)S(1)}, s32[8]{0:T(128)S(1)}, s32[128,256]{1,0:T(8,128)}, f32[2,3,513]{1,0,2:T(2,128)S(1)}, /*index=5*/f3...) while((s32[]{:T(128)}, f32[2,3,513]{2,0,1:T(2,128)S(1)}, ...), condition=%wide.region_10.11_spmd.clone, body=%wide.region_1.10_spmd.clone.sunk | while | flops 210304576 | bytes 3942428 | solution.py:90
  30.2 1.0 compare_and_fusion.2
  31.3 28.3 %gather_fusion = f32[4096,2,3]{2,1,0:T(2,128)} fusion(f32[2,3,513]{1,0,2:T(2,128)S(1)} %get-tuple-element.317, s32[4096]{0:T(1024)S(1)} %broadcast_clamp_fusion.2), kind=kCustom, calls=%fused_computation.clone.clone.1 | custom fusion | bytes 212992 | tf_op jit(solution)/shard_map/while/body/eval_jaxpr/jit(_take)/gather | solution.py:57
  59.6 5.7 copy.219
  67.0 16.7 %gather_fusion.1 = f32[4096]{0:T(1024)S(1)} fusion(f32[513]{0:T(1024)S(1)} %get-tuple-element.319, s32[4096]{0:T(1024)S(1)} %broadcast_clamp_fusion.2), kind=kCustom, calls=%fused_computation.1.clone.clone.1 | custom fusion | bytes 49152 | tf_op jit(solution)/shard_map/while/body/eval_jaxpr/gather | solution.py:52
  86.2 0.7 fusion.101
  88.5 4.2 fusion.102
  95.5 1.0 compare_and_fusion.2
  96.6 28.3 %gather_fusion = f32[4096,2,3]{2,1,0:T(2,128)} fusion(f32[2,3,513]{1,0,2:T(2,128)S(1)} %get-tuple-element.317, s32[4096]{0:T(1024)S(1)} %broadcast_clamp_fusion.2), kind=kCustom, calls=%fused_computation.clone.clone.1 | custom fusion | bytes 212992 | tf_op jit(solution)/shard_map/while/body/eval_jaxpr/jit(_take)/gather | solution.py:57
  124.9 5.7 copy.219
  132.3 16.7 %gather_fusion.1 = f32[4096]{0:T(1024)S(1)} fusion(f32[513]{0:T(1024)S(1)} %get-tuple-element.319, s32[4096]{0:T(1024)S(1)} %broadcast_clamp_fusion.2), kind=kCustom, calls=%fused_computation.1.clone.clone.1 | custom fusion | bytes 49152 | tf_op jit(solution)/shard_map/while/body/eval_jaxpr/gather | solution.py:52
  153.9 4.2 fusion.102
  161.3 1.0 compare_and_fusion.2
  162.4 28.3 %gather_fusion = f32[4096,2,3]{2,1,0:T(2,128)} fusion(f32[2,3,513]{1,0,2:T(2,128)S(1)} %get-tuple-element.317, s32[4096]{0:T(1024)S(1)} %broadcast_clamp_fusion.2), kind=kCustom, calls=%fused_computation.clone.clone.1 | custom fusion | bytes 212992 | tf_op jit(solution)/shard_map/while/body/eval_jaxpr/jit(_take)/gather | solution.py:57
  190.7 5.7 copy.219
  198.1 16.7 %gather_fusion.1 = f32[4096]{0:T(1024)S(1)} fusion(f32[513]{0:T(1024)S(1)} %get-tuple-element.319, s32[4096]{0:T(1024)S(1)} %broadcast_clamp_fusion.2), kind=kCustom, calls=%fused_computation.1.clone.clone.1 | custom fusion | bytes 49152 | tf_op jit(solution)/shard_map/while/body/eval_jaxpr/gather | solution.py:52
  217.3 0.7 fusion.101
  219.6 4.2 fusion.102
  227.0 1.0 compare_and_fusion.2
  228.1 28.3 %gather_fusion = f32[4096,2,3]{2,1,0:T(2,128)} fusion(f32[2,3,513]{1,0,2:T(2,128)S(1)} %get-tuple-element.317, s32[4096]{0:T(1024)S(1)} %broadcast_clamp_fusion.2), kind=kCustom, calls=%fused_computation.clone.clone.1 | custom fusion | bytes 212992 | tf_op jit(solution)/shard_map/while/body/eval_jaxpr/jit(_take)/gather | solution.py:57
  256.5 5.7 copy.219
  263.9 16.7 %gather_fusion.1 = f32[4096]{0:T(1024)S(1)} fusion(f32[513]{0:T(1024)S(1)} %get-tuple-element.319, s32[4096]{0:T(1024)S(1)} %broadcast_clamp_fusion.2), kind=kCustom, calls=%fused_computation.1.clone.clone.1 | custom fusion | bytes 49152 | tf_op jit(solution)/shard_map/while/body/eval_jaxpr/gather | solution.py:52
  285.4 4.2 fusion.102
  292.8 0.9 compare_and_fusion.2
  293.8 28.3 %gather_fusion = f32[4096,2,3]{2,1,0:T(2,128)} fusion(f32[2,3,513]{1,0,2:T(2,128)S(1)} %get-tuple-element.317, s32[4096]{0:T(1024)S(1)} %broadcast_clamp_fusion.2), kind=kCustom, calls=%fused_computation.clone.clone.1 | custom fusion | bytes 212992 | tf_op jit(solution)/shard_map/while/body/eval_jaxpr/jit(_take)/gather | solution.py:57
  322.1 5.7 copy.219
  329.5 16.7 %gather_fusion.1 = f32[4096]{0:T(1024)S(1)} fusion(f32[513]{0:T(1024)S(1)} %get-tuple-element.319, s32[4096]{0:T(1024)S(1)} %broadcast_clamp_fusion.2), kind=kCustom, calls=%fused_computation.1.clone.clone.1 | custom fusion | bytes 49152 | tf_op jit(solution)/shard_map/while/body/eval_jaxpr/gather | solution.py:52
  348.7 0.7 fusion.101
  351.1 4.2 fusion.102
  358.1 0.9 compare_and_fusion.2
  359.1 28.3 %gather_fusion = f32[4096,2,3]{2,1,0:T(2,128)} fusion(f32[2,3,513]{1,0,2:T(2,128)S(1)} %get-tuple-element.317, s32[4096]{0:T(1024)S(1)} %broadcast_clamp_fusion.2), kind=kCustom, calls=%fused_computation.clone.clone.1 | custom fusion | bytes 212992 | tf_op jit(solution)/shard_map/while/body/eval_jaxpr/jit(_take)/gather | solution.py:57
  387.4 5.7 copy.219
  394.8 16.7 %gather_fusion.1 = f32[4096]{0:T(1024)S(1)} fusion(f32[513]{0:T(1024)S(1)} %get-tuple-element.319, s32[4096]{0:T(1024)S(1)} %broadcast_clamp_fusion.2), kind=kCustom, calls=%fused_computation.1.clone.clone.1 | custom fusion | bytes 49152 | tf_op jit(solution)/shard_map/while/body/eval_jaxpr/gather | solution.py:52
  414.0 0.7 fusion.101
  416.4 4.2 fusion.102
  423.7 0.9 compare_and_fusion.2
  424.8 28.3 %gather_fusion = f32[4096,2,3]{2,1,0:T(2,128)} fusion(f32[2,3,513]{1,0,2:T(2,128)S(1)} %get-tuple-element.317, s32[4096]{0:T(1024)S(1)} %broadcast_clamp_fusion.2), kind=kCustom, calls=%fused_computation.clone.clone.1 | custom fusion | bytes 212992 | tf_op jit(solution)/shard_map/while/body/eval_jaxpr/jit(_take)/gather | solution.py:57
  453.1 5.7 copy.219
  460.5 16.7 %gather_fusion.1 = f32[4096]{0:T(1024)S(1)} fusion(f32[513]{0:T(1024)S(1)} %get-tuple-element.319, s32[4096]{0:T(1024)S(1)} %broadcast_clamp_fusion.2), kind=kCustom, calls=%fused_computation.1.clone.clone.1 | custom fusion | bytes 49152 | tf_op jit(solution)/shard_map/while/body/eval_jaxpr/gather | solution.py:52
  479.7 0.7 fusion.101
  482.0 4.2 fusion.102
  489.4 0.9 compare_and_fusion.2
  490.5 28.3 %gather_fusion = f32[4096,2,3]{2,1,0:T(2,128)} fusion(f32[2,3,513]{1,0,2:T(2,128)S(1)} %get-tuple-element.317, s32[4096]{0:T(1024)S(1)} %broadcast_clamp_fusion.2), kind=kCustom, calls=%fused_computation.clone.clone.1 | custom fusion | bytes 212992 | tf_op jit(solution)/shard_map/while/body/eval_jaxpr/jit(_take)/gather | solution.py:57
  518.8 5.7 copy.219
  526.2 16.7 %gather_fusion.1 = f32[4096]{0:T(1024)S(1)} fusion(f32[513]{0:T(1024)S(1)} %get-tuple-element.319, s32[4096]{0:T(1024)S(1)} %broadcast_clamp_fusion.2), kind=kCustom, calls=%fused_computation.1.clone.clone.1 | custom fusion | bytes 49152 | tf_op jit(solution)/shard_map/while/body/eval_jaxpr/gather | solution.py:52
  547.7 4.2 fusion.102
  552.8 7.7 %collective-permute-start.3 = (f32[1,2,3,128]{3,1,2,0:T(2,128)S(1)}, f32[1,2,3,128]{3,1,2,0:T(2,128)S(1)}, u32[]{:S(2)}, u32[]{:S(2)}) collective-permute-start(f32[1,2,3,128]{3,1,2,0:T(2,128)S(1)} %get-tuple-element.184), channel_id=1, source_target_pairs={{1,0},{2,1},{3,2},{4,3},{5,4},{6,5},{7,6},{8,7},{9,8},{10,9},{11,1... | collective-permute-start | bytes 9224 | tf_op jit(solution)/shard_map/ppermute | solution.py:29
  560.9 1.0 collective-permute-done.2
  562.2 4.9 scatter_fusion
  567.1 4.9 scatter_fusion.1
  572.6 1.0 reshape.411
  573.6 7.5 %all-to-all-start = ((f32[16,1,192]{2,1,0:T(1,128)}), f32[16,1,192]{2,1,0:T(1,128)S(1)}, u32[]{:S(2)}, u32[]{:S(2)}) async-start(f32[16,1,192]{2,1,0:T(1,128)} %reshape.411), calls=%async_computation | async-start | bytes 32768 | tf_op jit(solution)/shard_map/all_to_all | solution.py:165
  583.2 4.5 all-to-all-done
  590.8 4.7 all-to-all-start.2
  596.2 6.0 all-to-all-done.2
  (456 shorter events, 59.3 us)
Async XLA Ops:
  4.4 22.7 %collective-permute-start = (f32[1,2,4,128]{2,1,3,0:T(2,128)S(1)}, f32[1,2,4,128]{2,1,3,0:T(2,128)S(1)}, u32[]{:S(2)}, u32[]{:S(2)}) collective-permute-start(f32[1,2,4,128]{2,1,3,0:T(2,128)S(1)} %bitcast.133), channel_id=1, source_target_pairs={{0,1},{1,2},{2,3},{3,4},{4,5},{5,6},{6,7},{7,8},{8,9},{9,10},{10,1... | collective-permute-start | bytes 12296 | tf_op jit(solution)/shard_map/ppermute | solution.py:28
  5.2 21.9 %collective-permute-start.1 = (f32[1,2,4,128]{2,1,3,0:T(2,128)S(1)}, f32[1,2,4,128]{2,1,3,0:T(2,128)S(1)}, u32[]{:S(2)}, u32[]{:S(2)}) collective-permute-start(f32[1,2,4,128]{2,1,3,0:T(2,128)S(1)} %bitcast.134), channel_id=1, source_target_pairs={{1,0},{2,1},{3,2},{4,3},{5,4},{6,5},{7,6},{8,7},{9,8},{10,9},{11,1... | collective-permute-start | bytes 12296 | tf_op jit(solution)/shard_map/ppermute | solution.py:29
  16.0 557.6 %all-to-all-start.1 = ((f32[16,1,192]{2,1,0:T(1,128)}), f32[16,1,192]{2,1,0:T(1,128)S(1)}, u32[]{:S(2)}, u32[]{:S(2)}) async-start(f32[16,1,192]{2,1,0:T(1,128)} %reshape.409), calls=%async_computation.1 | async-start | bytes 32768 | tf_op jit(solution)/shard_map/all_to_all | solution.py:166
  27.6 544.8 %copy-start.2 = (f32[2,3,256]{2,0,1:T(2,128)S(1)}, f32[2,3,256]{2,0,1:T(2,128)}, u32[]{:S(2)}) copy-start(f32[2,3,256]{2,0,1:T(2,128)} %param.11) | copy-start | bytes 18436
  27.6 544.8 %copy-start.1 = (f32[2,3,256]{2,0,1:T(2,128)S(1)}, f32[2,3,256]{2,0,1:T(2,128)}, u32[]{:S(2)}) copy-start(f32[2,3,256]{2,0,1:T(2,128)} %param.10) | copy-start | bytes 18436
  67.0 18.1 %copy-start = (f32[2,512]{1,0:T(2,128)S(1)}, f32[2,512]{1,0:T(2,128)}, u32[]{:S(2)}) copy-start(f32[2,512]{1,0:T(2,128)} %get-tuple-element.318) | copy-start | bytes 12292 | tf_op jit(solution)/shard_map/while
  132.3 18.1 %copy-start = (f32[2,512]{1,0:T(2,128)S(1)}, f32[2,512]{1,0:T(2,128)}, u32[]{:S(2)}) copy-start(f32[2,512]{1,0:T(2,128)} %get-tuple-element.318) | copy-start | bytes 12292 | tf_op jit(solution)/shard_map/while
  198.1 18.1 %copy-start = (f32[2,512]{1,0:T(2,128)S(1)}, f32[2,512]{1,0:T(2,128)}, u32[]{:S(2)}) copy-start(f32[2,512]{1,0:T(2,128)} %get-tuple-element.318) | copy-start | bytes 12292 | tf_op jit(solution)/shard_map/while
  263.9 18.1 %copy-start = (f32[2,512]{1,0:T(2,128)S(1)}, f32[2,512]{1,0:T(2,128)}, u32[]{:S(2)}) copy-start(f32[2,512]{1,0:T(2,128)} %get-tuple-element.318) | copy-start | bytes 12292 | tf_op jit(solution)/shard_map/while
  329.5 18.1 %copy-start = (f32[2,512]{1,0:T(2,128)S(1)}, f32[2,512]{1,0:T(2,128)}, u32[]{:S(2)}) copy-start(f32[2,512]{1,0:T(2,128)} %get-tuple-element.318) | copy-start | bytes 12292 | tf_op jit(solution)/shard_map/while
  394.8 18.1 %copy-start = (f32[2,512]{1,0:T(2,128)S(1)}, f32[2,512]{1,0:T(2,128)}, u32[]{:S(2)}) copy-start(f32[2,512]{1,0:T(2,128)} %get-tuple-element.318) | copy-start | bytes 12292 | tf_op jit(solution)/shard_map/while
  460.5 18.1 %copy-start = (f32[2,512]{1,0:T(2,128)S(1)}, f32[2,512]{1,0:T(2,128)}, u32[]{:S(2)}) copy-start(f32[2,512]{1,0:T(2,128)} %get-tuple-element.318) | copy-start | bytes 12292 | tf_op jit(solution)/shard_map/while
  526.2 18.1 %copy-start = (f32[2,512]{1,0:T(2,128)S(1)}, f32[2,512]{1,0:T(2,128)}, u32[]{:S(2)}) copy-start(f32[2,512]{1,0:T(2,128)} %get-tuple-element.318) | copy-start | bytes 12292 | tf_op jit(solution)/shard_map/while
  552.6 9.3 %collective-permute-start.2 = (f32[1,2,3,128]{3,1,2,0:T(2,128)S(1)}, f32[1,2,3,128]{3,1,2,0:T(2,128)S(1)}, u32[]{:S(2)}, u32[]{:S(2)}) collective-permute-start(f32[1,2,3,128]{3,1,2,0:T(2,128)S(1)} %get-tuple-element.185), channel_id=1, source_target_pairs={{0,1},{1,2},{2,3},{3,4},{4,5},{5,6},{6,7},{7,8},{8,9},{9,10},{10,1... | collective-permute-start | bytes 9224 | tf_op jit(solution)/shard_map/ppermute | solution.py:28
  552.8 9.2 %collective-permute-start.3 = (f32[1,2,3,128]{3,1,2,0:T(2,128)S(1)}, f32[1,2,3,128]{3,1,2,0:T(2,128)S(1)}, u32[]{:S(2)}, u32[]{:S(2)}) collective-permute-start(f32[1,2,3,128]{3,1,2,0:T(2,128)S(1)} %get-tuple-element.184), channel_id=1, source_target_pairs={{1,0},{2,1},{3,2},{4,3},{5,4},{6,5},{7,6},{8,7},{9,8},{10,9},{11,1... | collective-permute-start | bytes 9224 | tf_op jit(solution)/shard_map/ppermute | solution.py:29
  573.6 14.2 %all-to-all-start = ((f32[16,1,192]{2,1,0:T(1,128)}), f32[16,1,192]{2,1,0:T(1,128)S(1)}, u32[]{:S(2)}, u32[]{:S(2)}) async-start(f32[16,1,192]{2,1,0:T(1,128)} %reshape.411), calls=%async_computation | async-start | bytes 32768 | tf_op jit(solution)/shard_map/all_to_all | solution.py:165
  590.8 11.5 %all-to-all-start.2 = ((f32[16,1,192]{2,1,0:T(1,128)}), f32[16,1,192]{2,1,0:T(1,128)S(1)}, u32[]{:S(2)}, u32[]{:S(2)}) async-start(f32[16,1,192]{2,1,0:T(1,128)} %reshape.413), calls=%async_computation.2 | async-start | bytes 32768 | tf_op jit(solution)/shard_map/all_to_all | solution.py:173
where the time goes:
time: 606 us; the launch traced here: 604 us
  local copies, waits for them, and re-layouts  443 us (73%)
  other arithmetic  44.4 us (7%)
  matrix products  39.6 us (7%)
  starting transfers between devices  37.2 us (6%)
  loops' own time  27.5 us (5%)
  waiting for transfers between devices  11.5 us (2%)
    gather x24, local copies, waits for them, and re-layouts, advance(): near = jnp.take(place, safe, axis=2)  274 us
    gather x24, local copies, waits for them, and re-layouts, advance(): hydro = spec_table[safe]  135 us
    dot_general x8, matrix products, advance(): jnp.dot(grad_near.reshape(rows, -1), select, precision=lax.Precision.HIGH...  33.8 us
    another operation x1, loops' own time, table_gradient(): total, _ = lax.scan(advance, jnp.zeros_like(place), starts)  27.5 us
    ppermute x2, starting transfers between devices, extended(): after = lax.ppermute(first, axis, down)  16.6 us
  transfers between devices with their start and end apart: 7, of which 3 were waited for; matrix products, arithmetic and copies ran while one was open for 86% of the time, Pallas kernels for 0%

commit v1 on v0

v1 whole, which is shorter than its diff:
```python
import functools
import math

import jax
import jax.numpy as jnp
import numpy as np
from jax import lax
from jax.experimental import pallas as pl
from jax.experimental.pallas import tpu as pltpu
from jax.sharding import PartitionSpec as P

BEADS = 32
NRAD = 32
HI = lax.Precision.HIGHEST
F32 = jnp.float32
BF16 = jnp.bfloat16
WHOLE = pl.BlockSpec(memory_space=pltpu.VMEM)


def step_tables():
    index = np.arange(BEADS)
    angle = 2.0 * np.pi * np.outer(index, index) / BEADS
    modes = np.where(
        index == 0,
        1.0 / np.sqrt(BEADS),
        np.where(
            2 * index < BEADS,
            np.sqrt(2.0 / BEADS) * np.cos(angle),
            np.where(
                2 * index == BEADS,
                np.cos(angle) / np.sqrt(BEADS),
                np.sqrt(2.0 / BEADS) * np.sin(angle),
            ),
        ),
    )
    freq = 2.0 * np.sin(np.pi * index / BEADS)
    keep = np.exp(-0.25 * np.where(index == 0, 0.2, 2.0 * freq))
    fresh = np.sqrt(1.0 - keep * keep)
    cosine, sine = np.cos(0.5 * freq), np.sin(0.5 * freq)
    spread = np.where(index == 0, 0.5, sine / np.where(index == 0, 1.0, freq))
    kinds = [
        (0, (modes * cosine) @ modes.T),
        (1, -(modes * (keep * freq * sine)) @ modes.T),
        (0, (modes * (spread * keep)) @ modes.T),
        (1, (modes * (keep * keep * cosine)) @ modes.T),
        (0, modes * (spread * fresh)),
        (1, modes * (keep * cosine * fresh)),
        (1, modes * fresh),
    ]
    base = np.zeros((16, 16, 2, 2, 3, 2, 2, 7, 8))
    for kind, (output, matrix) in enumerate(kinds):
        blocks = matrix.reshape(16, 2, 16, 2)
        for sender in range(16):
            for half in range(2):
                for b in range(2):
                    for c in range(3):
                        base[sender, :, half, output, c, :, half, kind, c * 2 + b] = blocks[
                            :, :, sender, b
                        ]
    return base.reshape(16, 384, 112).astype(np.float32)


STEP_TABLE = step_tables()


def lanes(row, count=8):
    return jnp.broadcast_to(row, (count, 128))


def take(chunk, index):
    return jnp.take_along_axis(chunk, index, axis=1, mode="promise_in_bounds")


def take_pair(low, high, index):
    local = index & 127
    return jnp.where(index < 128, take(low, local), take(high, local))


def halves(pieces):
    return jnp.concatenate([p[:, 0:128] for p in pieces] + [p[:, 128:256] for p in pieces], axis=0)


def fetch_all(sources, targets, semaphores):
    copies = [
        pltpu.make_async_copy(source, target, semaphores.at[i])
        for i, (source, target) in enumerate(zip(sources, targets))
    ]
    for copy in copies:
        copy.start()
    for copy in copies:
        copy.wait()


def pack_kernel(positions_hbm, species_hbm, ghost_hbm, out_ref, positions, species, ghost, sems):
    fetch_all((positions_hbm, species_hbm, ghost_hbm), (positions, species, ghost), sems)
    out_ref[...] = jnp.concatenate(
        [positions[c] for c in range(3)]
        + [species[...].astype(F32)]
        + [jnp.concatenate([ghost[0:1, :], ghost[1:2, :]], axis=1).astype(F32)],
        axis=0,
    )


def split(value):
    coarse = value.astype(BF16)
    return coarse, (value - coarse.astype(F32)).astype(BF16)


def dot3(left, right):
    a, b = split(left)
    c, d = split(right)
    dot = functools.partial(jnp.dot, preferred_element_type=F32)
    return dot(a, c) + (dot(a, d) + dot(b, c))


def odd_slab():
    return jnp.full((8, 128), lax.axis_index("space") % 2, jnp.int32) == 1


def column_sums(values):
    row = lax.broadcasted_iota(jnp.int32, (8, 128), 0)
    top = row < 4
    four = [
        jnp.where(top, values[k], values[k + 4])
        + pltpu.roll(jnp.where(top, values[k + 4], values[k]), 4, 0)
        for k in range(4)
    ]
    top = (row & 3) < 2
    two = [
        jnp.where(
            top, four[k] + pltpu.roll(four[k], 6, 0), four[k + 2] + pltpu.roll(four[k + 2], 2, 0)
        )
        for k in range(2)
    ]
    top = (row & 1) < 1
    return jnp.where(top, two[0] + pltpu.roll(two[0], 7, 0), two[1] + pltpu.roll(two[1], 1, 0))


def taps():
    away = (lax.broadcasted_iota(jnp.int32, (8, 128), 0) - 4).astype(F32)
    return jnp.exp(away * away * -0.5)


def quad_kernel(sparse_ref, coef_ref, quad_ref):
    sparse = sparse_ref[...]
    basis = sparse * lax.rsqrt(jnp.sum(sparse * sparse, axis=0, keepdims=True) + 1e-6)
    scaled = jnp.concatenate([basis * coef_ref[0:1, :], basis * coef_ref[1:2, :]], axis=0)
    quad_ref[...] = lax.dot_general(
        scaled, basis, (((1,), (1,)), ((), ())), precision=HI, preferred_element_type=F32
    )


def scatter(slots, hot_of, value_of):
    return lax.dot_general(
        jnp.concatenate([hot_of(slot) for slot in range(slots)], axis=1),
        jnp.concatenate([value_of(slot) for slot in range(slots)], axis=1),
        (((1,), (1,)), ((), ())),
        preferred_element_type=F32,
    ).T


def levels(count, wide):
    return lax.broadcasted_iota(jnp.int32, (count, wide), 0).astype(F32).astype(BF16)


def one_hot(row, level):
    count, wide = level.shape
    entry = jnp.broadcast_to(row, (16, wide)).astype(BF16)
    one = jnp.ones((16, wide), BF16)
    return jnp.concatenate(
        [
            jnp.where(entry == level[r * 16 : r * 16 + 16], one, jnp.zeros_like(one))
            for r in range(count // 16)
        ],
        axis=0,
    )


def coded(full, row, codes):
    wide = full.shape[1]
    coarse = full.astype(BF16).astype(F32)
    two = jnp.concatenate([coarse, full - coarse], axis=0).astype(BF16)
    code = jnp.broadcast_to(row, (16, wide)).astype(BF16)
    return jnp.concatenate(
        [
            jnp.where(code == jnp.full((16, wide), c, BF16), two, jnp.zeros_like(two))
            for c in range(codes)
        ],
        axis=0,
    )


def joined(sums):
    grad = jnp.concatenate([sums[0:8] + sums[8:16], sums[16:24] + sums[24:32]], axis=1)
    return jnp.where(lax.broadcasted_iota(jnp.int32, grad.shape, 0) < 6, grad, 0.0)


def force_kernel(
    own_ref,
    far_ref,
    close_ref,
    nbr_ref,
    quad_ref,
    to_far_ref,
    to_near_ref,
    grad_ref,
    v_ref,
    index_ref,
    central_ref,
    low_ref,
    code_ref,
    src_ref,
    hyd_ref,
    t_ref,
    geo_ref,
    e_ref,
    p_ref,
    desc_ref,
    g_ref,
):
    odd = odd_slab()

    far = far_ref[...]
    close = close_ref[...]
    far_low, far_high = (lanes(far[7:8, h * 128 : h * 128 + 128]) for h in range(2))
    close_low, close_high = (lanes(close[7:8, h * 128 : h * 128 + 128]) for h in range(2))
    far_pick = jnp.where(odd, far_low, far_high).astype(jnp.int32)
    close_pick = jnp.where(odd, close_high, close_low).astype(jnp.int32)
    far = take_pair(far[:, 0:128], far[:, 128:256], far_pick)
    close = take_pair(close[:, 0:128], close[:, 128:256], close_pick)
    own = own_ref[...]
    listed = own[7:8].astype(jnp.int32)
    chunks = [
        own[:, 0:128],
        own[:, 128:256],
        jnp.where(odd, close, far),
        jnp.where(odd, far, close),
    ]
    for c in range(4):
        for r in range(7):
            src_ref[c * 7 + r] = lanes(chunks[c][r : r + 1])

    for half in range(2):
        cols = slice(half * 128, half * 128 + 128)
        pick = lanes(listed[:, cols])
        central_ref[:, cols] = take_pair(chunks[0], chunks[1], pick)

        def gather(s, carry, half=half, cols=cols, pick=pick):
            rows = pl.ds(pl.multiple_of(s * 8, 8), 8)
            index = take_pair(nbr_ref[rows, 0:128], nbr_ref[rows, 128:256], pick)
            index_ref[half, rows, :] = index
            local = index & 127
            first = index < 128
            own = index < 256
            live = index < 512
            low_ref[half, rows, :] = (index & 63).astype(F32)
            code_ref[half, rows, :] = jnp.where(live & ~own, local >> 6, 2).astype(F32)

            def fetch(r):
                mine = jnp.where(first, take(src_ref[r], local), take(src_ref[7 + r], local))
                return jnp.where(own, mine, take(src_ref[14 + half * 7 + r], local))

            hyd_ref[half, rows, :] = fetch(6)
            for b in range(2):
                bl = b * 2 + half
                delta = [
                    fetch(c * 2 + b) - lanes(central_ref[c * 2 + b : c * 2 + b + 1, cols])
                    for c in range(3)
                ]
                square = delta[0] * delta[0] + delta[1] * delta[1] + delta[2] * delta[2] + 0.25
                inverse = lax.rsqrt(square)
                ratio = square * (1.0 / 25.0)
                keep = jnp.where(live & (ratio < 1.0), 1.0 - ratio, 0.0)
                reach = jnp.minimum(square * inverse * 6.4, 32.0)
                t_ref[bl, rows, :] = reach
                for c in range(3):
                    geo_ref[bl, c, rows, :] = delta[c]
                geo_ref[bl, 3, rows, :] = inverse
                geo_ref[bl, 4, rows, :] = keep
                e_ref[bl, 0, rows, :] = jnp.exp(reach)
                e_ref[bl, 1, rows, :] = jnp.exp(-reach)
            return carry

        lax.fori_loop(0, 16, gather, 0, unroll=16)

    tap = taps()

    def radial(bl, carry):
        half = bl & 1
        for a in range(4):
            center = 8.0 * a + 4.0

            def step(s, total, center=center, a=a):
                rows = pl.ds(pl.multiple_of(s * 8, 8), 8)
                tau = t_ref[bl, rows, :] - center
                keep = geo_ref[bl, 4, rows, :]
                hydro = hyd_ref[half, rows, :]
                up = e_ref[bl, 0, rows, :] * math.exp(-center)
                down = e_ref[bl, 1, rows, :] * math.exp(center)
                tower = [None] * 8
                tower[4] = jnp.exp(tau * tau * -0.5) * (keep * keep)
                for m in range(5, 8):
                    tower[m] = tower[m - 1] * up
                for m in range(3, -1, -1):
                    tower[m] = tower[m + 1] * down
                new = []
                for m in range(8):
                    p_ref[bl, a * 8 + m, rows, :] = tower[m]
                    new.append(total[2 * m] + tower[m])
                    new.append(total[2 * m + 1] + tower[m] * hydro)
                return tuple(new)

            zero = jnp.zeros((8, 128), F32)
            total = lax.fori_loop(0, 16, step, (zero,) * 16, unroll=16)
            every = column_sums(total[0::2])
            hydrogen = column_sums(total[1::2])
            desc_ref[bl, a * 8 : a * 8 + 8, :] = (every - hydrogen) * tap
            desc_ref[bl, NRAD + a * 8 : NRAD + a * 8 + 8, :] = hydrogen * tap
        return carry

    lax.fori_loop(0, 4, radial, 0, unroll=4)

    desc = [desc_ref[bl] for bl in range(4)]
    norm = [lax.rsqrt(jnp.sum(d * d, axis=0, keepdims=True) + 1e-6) for d in desc]
    unit = [d * n for d, n in zip(desc, norm)]
    turned = dot3(quad_ref[...], jnp.concatenate(unit, axis=1))
    tap = jnp.concatenate([taps()] * 8, axis=0)
    for bl in range(4):
        half = bl & 1
        heavy = central_ref[6:7, half * 128 : half * 128 + 128] < 0.5
        mine = turned[:, bl * 128 : bl * 128 + 128]
        slope = jnp.where(heavy, mine[0:64], mine[64:128])
        along = jnp.sum(slope * unit[bl], axis=0, keepdims=True)
        g_ref[bl] = (2.0 * norm[bl]) * (slope - unit[bl] * along) * tap

    group = 4
    grad_ref[6:8, :] = jnp.zeros((2, 256), F32)
    for b in range(2):
        for half in range(2):
            bl = b * 2 + half

            def back(s, total, b=b, bl=bl, half=half):
                start = pl.multiple_of(s * (8 * group), 8 * group)
                rows = [pl.ds(start + 8 * q, 8) for q in range(group)]
                hydro = [hyd_ref[half, r, :] > 0.5 for r in rows]
                plain = [None] * group
                ramp = [None] * group
                for k in range(NRAD - 1, -1, -1):
                    oxygen = lanes(g_ref[bl, k : k + 1, :])
                    hydrogen = lanes(g_ref[bl, NRAD + k : NRAD + k + 1, :])
                    for q in range(group):
                        x = p_ref[bl, k, rows[q], :] * jnp.where(hydro[q], hydrogen, oxygen)
                        plain[q] = x if k == NRAD - 1 else plain[q] + x
                        ramp[q] = plain[q] if k == NRAD - 1 else ramp[q] + plain[q]
                total = list(total)
                for q in range(group):
                    reach = t_ref[bl, rows[q], :]
                    inverse = geo_ref[bl, 3, rows[q], :]
                    keep = geo_ref[bl, 4, rows[q], :]
                    inside = keep > 0.0
                    fade = jnp.where(inside, (-4.0 / 25.0) / jnp.where(inside, keep, 1.0), 0.0)
                    slope = (reach + 1.0) * plain[q] - ramp[q]
                    pull = plain[q] * fade - 6.4 * slope * inverse
                    for c in range(3):
                        part = pull * geo_ref[bl, c, rows[q], :]
                        total[c] = total[c] + part
                        v_ref[half, pl.ds((start + 8 * q) * 8 + c * 2 + b, 8, stride=8), :] = part
                return tuple(total)

            zero = jnp.zeros((8, 128), F32)
            total = lax.fori_loop(0, 16 // group, back, (zero,) * 3, unroll=4)
            for c in range(3):
                grad_ref[c * 2 + b : c * 2 + b + 1, half * 128 : half * 128 + 128] = -jnp.sum(
                    total[c], axis=0, keepdims=True
                )

    copies = []
    level = levels(64, 128)
    for half in range(2):
        sums = scatter(
            128,
            lambda slot, half=half: one_hot(low_ref[half, pl.ds(slot, 1), :], level),
            lambda slot, half=half: coded(
                v_ref[half, pl.ds(slot * 8, 8), :],
                code_ref[half, pl.ds(slot, 1), :],
                2,
            ),
        )
        copies.append(joined(sums))
    to_far_ref[...] = jnp.where(odd, copies[1], copies[0])
    to_near_ref[...] = jnp.where(odd, copies[0], copies[1])


def push_rows(grad, packet_ref):
    push = grad * -0.25
    mass = jnp.where(packet_ref[6:7, :] > 0.5, 1.0, 16.0)
    none = jnp.zeros((8, 256), F32)
    return halves([none, none, push / mass, push, none, none, none])


def base_rows(own, momenta_ref, noise_ref):
    light = own[6:7] > 0.5
    mass = jnp.where(light, 1.0, 16.0)
    root = jnp.where(light, 1.0, 4.0)
    blank = jnp.zeros((2, 256), F32)
    moment = jnp.concatenate([momenta_ref[c] for c in range(3)] + [blank], axis=0)
    first = jnp.concatenate([noise_ref[c] for c in range(3)] + [blank], axis=0)
    second = jnp.concatenate([noise_ref[3 + c] for c in range(3)] + [blank], axis=0)
    return halves(
        [own, own * mass, moment / mass, moment, first / root, first * root, second * root]
    )


def places(packet_ref):
    listed = packet_ref[7:8, :].astype(jnp.int32)
    same = lax.broadcasted_iota(jnp.int32, (256, 256), 0) == listed
    place = lax.broadcasted_iota(jnp.int32, (8, 256), 1).astype(F32).astype(BF16)
    return lax.dot_general(
        place,
        jnp.where(same, 1.0, 0.0).astype(BF16),
        (((1,), (1,)), ((), ())),
        preferred_element_type=F32,
    ).astype(jnp.int32)


def gather_kernel(
    v_ref,
    index_ref,
    grad_ref,
    packet_ref,
    momenta_ref,
    noise_ref,
    table_ref,
    own_ref,
    sum_ref,
    back_ref,
):
    back_ref[...] = places(packet_ref)
    level = levels(128, 256)
    wide = lambda pick, slot: jnp.concatenate([pick(h, slot) for h in range(2)], axis=1)
    index = lambda slot: wide(lambda h, s: index_ref[h, pl.ds(s, 1), :], slot)
    sums = scatter(
        128,
        lambda slot: one_hot((index(slot) & 127).astype(F32), level),
        lambda slot: coded(
            wide(lambda h, s: v_ref[h, pl.ds(s * 8, 8), :], slot),
            (index(slot) >> 7).astype(F32),
            2,
        ),
    )
    passed = joined(sums)
    central = jnp.concatenate(
        [
            take_pair(grad_ref[:, 0:128], grad_ref[:, 128:256], back_ref[:, 0:128]),
            take_pair(grad_ref[:, 0:128], grad_ref[:, 128:256], back_ref[:, 128:256]),
        ],
        axis=1,
    )
    own = passed + central
    own_ref[...] = own
    sum_ref[...] = jnp.dot(
        table_ref[...],
        base_rows(packet_ref[...], momenta_ref, noise_ref) + push_rows(own, packet_ref),
        precision=HI,
        preferred_element_type=F32,
    )


def combine_kernel(
    far_ref, near_ref, back_ref, packet_ref, table_ref, own_ref, base_ref, forces_ref, send_ref
):
    odd = odd_slab()
    low = jnp.where(odd, near_ref[...], far_ref[...])
    high = jnp.where(odd, far_ref[...], near_ref[...])
    passed = jnp.concatenate(
        [take_pair(low, high, back_ref[:, 0:128]), take_pair(low, high, back_ref[:, 128:256])],
        axis=1,
    )
    forces = -own_ref[...] - passed
    for c in range(3):
        forces_ref[c] = forces[c * 2 : c * 2 + 2]
    send_ref[...] = base_ref[...] + dot3(table_ref[...], push_rows(passed, packet_ref))


def finish_kernel(parts_ref, positions_ref, momenta_ref):
    total = parts_ref[0]
    for d in range(1, 16):
        total = total + parts_ref[d]
    for half in range(2):
        cols = slice(half * 128, half * 128 + 128)
        for c in range(3):
            row = half * 12 + c * 2
            positions_ref[c, :, cols] = total[row : row + 2]
            momenta_ref[c, :, cols] = total[row + 6 : row + 8]


def call(kernel, shapes, count, name, mib=1, scratch=(), ints=(), fetched=()):
    buffers = [pltpu.VMEM(shape, F32) for shape in scratch]
    buffers += [pltpu.VMEM(value.shape, value.dtype) for value in fetched]
    if fetched:
        buffers.append(pltpu.SemaphoreType.DMA((len(fetched),)))
    return pl.pallas_call(
        kernel,
        out_shape=[
            jax.ShapeDtypeStruct(shape, jnp.int32 if i in ints else F32)
            for i, shape in enumerate(shapes)
        ],
        in_specs=[WHOLE] * count + [pl.BlockSpec(memory_space=pltpu.HBM)] * len(fetched),
        out_specs=[WHOLE] * len(shapes),
        scratch_shapes=buffers,
        compiler_params=pltpu.CompilerParams(vmem_limit_bytes=mib * 1024 * 1024),
        name=name,
    )


def per_device(
    positions, momenta, species, neighbours, ghost_index, sparse_points, coefficients, noise
):
    size = lax.axis_size("space")
    close = [(i, i ^ 1) for i in range(size)]
    distant = [(i, (i + 1) % size if i % 2 else (i - 1) % size) for i in range(size)]
    turn = lambda value: jnp.transpose(value, (1, 0, 2))
    kind = species.reshape(1, 256)
    own = (turn(positions), kind, ghost_index)
    (packet,) = call(pack_kernel, [(8, 256)], 0, "pack", fetched=own)(*own)
    far = lax.ppermute(packet, "space", distant)
    near = lax.ppermute(packet, "space", close)
    table = lax.dynamic_index_in_dim(
        jnp.asarray(STEP_TABLE), lax.axis_index("bead"), 0, keepdims=False
    )
    (quad,) = call(quad_kernel, [(128, 64)], 2, "quad", 2)(sparse_points, coefficients)
    to_far, to_near, grad, pulls, index = table_gradient(packet, far, near, neighbours, quad)
    from_far = lax.ppermute(to_far, "space", distant)
    from_near = lax.ppermute(to_near, "space", close)
    own_grad, summed, back = call(
        gather_kernel, [(8, 256), (384, 128), (8, 256)], 7, "gather", 8, ints=(2,)
    )(pulls, index, grad, packet, turn(momenta), turn(noise), table)
    forces, send = call(combine_kernel, [(3, 2, 256), (384, 128)], 7, "combine", 4)(
        from_far, from_near, back, packet, table, own_grad, summed
    )
    parts = lax.all_to_all(send.reshape(16, 24, 128), "bead", split_axis=0, concat_axis=0, tiled=True)
    new_positions, new_momenta = call(finish_kernel, [(3, 2, 256)] * 2, 1, "finish")(parts)
    return (turn(new_positions), turn(new_momenta), turn(forces))


def table_gradient(*args):
    return call(
        force_kernel,
        [(8, 128), (8, 128), (8, 256), (2, 1024, 128), (2, 128, 128)],
        5,
        "force",
        20,
        scratch=[
            (8, 256),
            (2, 128, 128),
            (2, 128, 128),
            (28, 8, 128),
            (2, 128, 128),
            (4, 128, 128),
            (4, 5, 128, 128),
            (4, 2, 128, 128),
            (4, 32, 128, 128),
            (4, 64, 128),
            (4, 64, 128),
        ],
        ints=(4,),
    )(*args)


def solution(mesh):
    placed = (
        P("bead", None, "space"),
        P("bead", None, "space"),
        P("space"),
        P(None, "space"),
        P(None, "space"),
        P(),
        P(),
        P("bead", None, "space"),
    )
    return jax.shard_map(
        per_device,
        mesh=mesh,
        in_specs=placed,
        out_specs=(P("bead", None, "space"), P("bead", None, "space"), P("bead", None, "space")),
        check_vma=False,
    )
```

time: 606 us -> 51.4 us (0.08)
  the two profiles are of different devices: /device:TPU:8 before, /device:TPU:1 now
where the time goes in v1:
time: 51.4 us; the launch traced here: 51 us
  starting transfers between devices  18.2 us (35%)
  blocking collectives  14.6 us (28%)
  Pallas kernels  10.6 us (21%)
  local copies, waits for them, and re-layouts  6.86 us (13%)
  between operations  0.72 us (1%)
    all_to_all x1, blocking collectives, per_device(): lax.all_to_all(send.reshape(16, 24, 128), 'bead', split_axis=0, concat_ax...  14.6 us
    unnamed x16, local copies, waits for them, and re-layouts  5.92 us
    pallas_call x1, Pallas kernels, table_gradient(): call(force_kernel, [(8, 128), (8, 128), (8, 256), (2, 1024, 128), (2, 128...  5.89 us
    ppermute x1, starting transfers between devices, per_device(): far = lax.ppermute(packet, 'space', distant)  5.16 us
    ppermute x1, starting transfers between devices, per_device(): from_far = lax.ppermute(to_far, 'space', distant)  5.03 us
    ppermute x1, starting transfers between devices, per_device(): from_near = lax.ppermute(to_near, 'space', close)  4.71 us
    ppermute x1, starting transfers between devices, per_device(): near = lax.ppermute(packet, 'space', close)  3.33 us
    pallas_call x1, Pallas kernels, per_device(): call(gather_kernel, [(8, 256), (384, 128), (8, 256)], 7, 'gather', 8, int...  2.94 us
  transfers between devices with their start and end apart: 4, of which 0 were waited for; matrix products, arithmetic and copies ran while one was open for 2% of the time, Pallas kernels for 7%

profile of v1, /device:TPU:1, one launch (start us, length us, event | category | flops | bytes accessed | tf_op | source)
XLA Modules:
  0.0 51.0 jit_solution(4664731952091318585)
XLA Ops:
  0.6 0.0 copy-start.4
  0.6 0.7 %copy-done.4 = f32[2,3,256]{2,0,1:T(2,128)S(1)} copy-done((f32[2,3,256]{2,0,1:T(2,128)S(1)}, f32[2,3,256]{2,0,1:T(2,128)}, u32[]{:S(2)}) %copy-start.4) | copy-done | bytes 6168
  1.3 0.0 copy-start.6
  1.3 0.7 %copy-done.6 = s32[256]{0:T(256)S(1)} copy-done((s32[256]{0:T(256)S(1)}, s32[256]{0:T(256)}, u32[]{:S(2)}) %copy-start.6) | copy-done | bytes 1048
  2.0 0.0 copy-start.7
  2.0 0.7 %copy-done.7 = s32[2,128]{1,0:T(2,128)S(1)} copy-done((s32[2,128]{1,0:T(2,128)S(1)}, s32[2,128]{1,0:T(2,128)}, u32[]{:S(2)}) %copy-start.7) | copy-done | bytes 1048
  2.7 3.3 %collective-permute-start.1 = (f32[8,256]{1,0:T(8,128)S(1)}, f32[8,256]{1,0:T(8,128)S(1)}, u32[]{:S(2)}, u32[]{:S(2)}) collective-permute-start(f32[8,256]{1,0:T(8,128)S(1)} %pack.1.own_ref.packet_ref), channel_id=1, source_target_pairs={{0,1},{1,0},{2,3},{3,2},{4,5},{5,4},{6,7},{7,6},{8,9},{9,8},{10,11... | collective-permute-start | bytes 24584 | tf_op jit(solution)/shard_map/ppermute | solution.py:527
  6.1 5.2 %collective-permute-start = (f32[8,256]{1,0:T(8,128)S(1)}, f32[8,256]{1,0:T(8,128)S(1)}, u32[]{:S(2)}, u32[]{:S(2)}) collective-permute-start(f32[8,256]{1,0:T(8,128)S(1)} %pack.1.own_ref.packet_ref), channel_id=1, source_target_pairs={{0,15},{1,2},{2,1},{3,4},{4,3},{5,6},{6,5},{7,8},{8,7},{9,10},{10,... | collective-permute-start | bytes 24584 | tf_op jit(solution)/shard_map/ppermute | solution.py:526
  11.2 0.0 copy-start.1
  11.2 0.9 %copy-done.1 = f32[64,512]{1,0:T(8,128)S(1)} copy-done((f32[64,512]{1,0:T(8,128)S(1)}, f32[64,512]{1,0:T(8,128)}, u32[]{:S(2)}) %copy-start.1) | copy-done | bytes 131096
  12.1 0.0 copy-start.5
  12.1 0.7 %copy-done.5 = f32[2,512]{1,0:T(2,128)S(1)} copy-done((f32[2,512]{1,0:T(2,128)S(1)}, f32[2,512]{1,0:T(2,128)}, u32[]{:S(2)}) %copy-start.5) | copy-done | bytes 4120
  12.8 0.4 quad.1.quad_ref
  13.2 0.0 collective-permute-done.1.close_ref
  13.2 0.0 collective-permute-done.far_ref
  13.2 0.0 copy-start
  13.2 0.9 %copy-done = s32[128,256]{1,0:T(8,128)S(1)} copy-done((s32[128,256]{1,0:T(8,128)S(1)}, s32[128,256]{1,0:T(8,128)}, u32[]{:S(2)}) %copy-start) | copy-done | bytes 131096
  14.1 5.9 %force.1 = (f32[8,128]{1,0:T(8,128)S(1)}, f32[8,128]{1,0:T(8,128)S(1)}, f32[8,256]{1,0:T(8,128)S(1)}, f32[2,1024,128]{2,1,0:T(8,128)S(1)}, s32[2,128,128]{2,1,0:T(8,128)S(1)}) custom-call(f32[8,256]{1,0:T(8,128)S(1)} %pack.1.own_ref.packet_ref, f32[8,256]{1,0:T(8,128)S(1)} %collective-permute-done.far_ref, f32[8,256]{1,0:T(8,128)S(1)} %collective-permute-done.1.close_ref, ...), custom_call_target="tpu_custom_call" | custom-call | tf_op jit(solution)/shard_map/force/pallas_call | solution.py:547
  20.0 5.0 %collective-permute-start.2 = (f32[8,128]{1,0:T(8,128)S(1)}, f32[8,128]{1,0:T(8,128)S(1)}, u32[]{:S(2)}, u32[]{:S(2)}) collective-permute-start(f32[8,128]{1,0:T(8,128)S(1)} %get-tuple-element.15), channel_id=1, source_target_pairs={{0,15},{1,2},{2,1},{3,4},{4,3},{5,6},{6,5},{7,8},{8,7},{9,10},{10,... | collective-permute-start | bytes 12296 | tf_op jit(solution)/shard_map/ppermute | solution.py:533
  25.1 4.7 %collective-permute-start.3 = (f32[8,128]{1,0:T(8,128)S(1)}, f32[8,128]{1,0:T(8,128)S(1)}, u32[]{:S(2)}, u32[]{:S(2)}) collective-permute-start(f32[8,128]{1,0:T(8,128)S(1)} %get-tuple-element.16), channel_id=1, source_target_pairs={{0,1},{1,0},{2,3},{3,2},{4,5},{5,4},{6,7},{7,6},{8,9},{9,8},{10,11... | collective-permute-start | bytes 12296 | tf_op jit(solution)/shard_map/ppermute | solution.py:534
  29.8 0.9 %dynamic-slice_bitcast_fusion.table_ref = f32[384,112]{1,0:T(8,128)S(1)} fusion(f32[16,384,112]{2,1,0:T(8,128)} %constant.13.clone, s32[]{:T(128)S(6)} %select_n.4), kind=kLoop, calls=%fused_computation | loop fusion | bytes 344068 | tf_op jit(solution)/shard_map/jit(dynamic_index_in_dim)/squeeze | solution.py:528
  30.7 0.0 copy-start.2
  30.7 0.7 %copy-done.2 = f32[2,6,256]{2,0,1:T(2,128)S(1)} copy-done((f32[2,6,256]{2,0,1:T(2,128)S(1)}, f32[2,6,256]{2,0,1:T(2,128)}, u32[]{:S(2)}) %copy-start.2) | copy-done | bytes 12312
  31.4 0.0 copy-start.3
  31.4 0.7 %copy-done.3 = f32[2,3,256]{2,0,1:T(2,128)S(1)} copy-done((f32[2,3,256]{2,0,1:T(2,128)S(1)}, f32[2,3,256]{2,0,1:T(2,128)}, u32[]{:S(2)}) %copy-start.3) | copy-done | bytes 6168
  32.1 2.9 %gather.1 = (f32[8,256]{1,0:T(8,128)S(1)}, f32[384,128]{1,0:T(8,128)S(1)}, s32[8,256]{1,0:T(8,128)S(1)}) custom-call(f32[2,1024,128]{2,1,0:T(8,128)S(1)} %get-tuple-element.17.v_ref, s32[2,128,128]{2,1,0:T(8,128)S(1)} %get-tuple-element.18.index_ref, f32[8,256]{1,0:T(8,128)S(1)} %get-tuple-element.19.grad_ref, f32[8,256]{1,0:T(8,128)S(1)} %pack.1.own_ref.packet_ref, ...), custom_call_target="tpu_custom_call" | custom-call | tf_op jit(solution)/shard_map/gather/pallas_call | solution.py:535
  35.1 0.0 collective-permute-done.2.far_ref
  35.1 0.0 collective-permute-done.3.near_ref
  35.1 0.7 %combine.1 = (f32[3,2,256]{2,1,0:T(2,128)}, f32[384,128]{1,0:T(8,128)S(1)}) custom-call(f32[8,128]{1,0:T(8,128)S(1)} %collective-permute-done.2.far_ref, f32[8,128]{1,0:T(8,128)S(1)} %collective-permute-done.3.near_ref, s32[8,256]{1,0:T(8,128)S(1)} %get-tuple-element.20.back_ref, f32[8,256]{1,0:T(8,128)S(1)} %pack.1.own_ref.packet_ref, ...), custom_call_target="tpu_custom_call" | custom-call | tf_op jit(solution)/shard_map/combine/pallas_call | solution.py:538
  35.8 14.6 %all_to_all.5.parts_ref = f32[16,24,128]{2,1,0:T(8,128)S(1)} all-to-all(f32[16,24,128]{2,1,0:T(8,128)S(1)} %bitcast.10), channel_id=1, replica_groups=mesh['bead'=16,'space'=16] {'bead'}, dimensions={0} | all-to-all | bytes 393216 | tf_op jit(solution)/shard_map/all_to_all | solution.py:541
  50.4 0.6 %finish.1 = (f32[3,2,256]{2,1,0:T(2,128)}, f32[3,2,256]{2,1,0:T(2,128)}) custom-call(f32[16,24,128]{2,1,0:T(8,128)S(1)} %all_to_all.5.parts_ref), custom_call_target="tpu_custom_call" | custom-call | tf_op jit(solution)/shard_map/finish/pallas_call | solution.py:542
  (1 shorter events, 0.0 us)
Async XLA Ops:
  0.6 0.7 %copy-start.4 = (f32[2,3,256]{2,0,1:T(2,128)S(1)}, f32[2,3,256]{2,0,1:T(2,128)}, u32[]{:S(2)}) copy-start(f32[2,3,256]{2,0,1:T(2,128)} %param.9) | copy-start | bytes 18436
  1.3 0.7 %copy-start.6 = (s32[256]{0:T(256)S(1)}, s32[256]{0:T(256)}, u32[]{:S(2)}) copy-start(s32[256]{0:T(256)} %param.11) | copy-start | bytes 3076
  2.0 0.7 %copy-start.7 = (s32[2,128]{1,0:T(2,128)S(1)}, s32[2,128]{1,0:T(2,128)}, u32[]{:S(2)}) copy-start(s32[2,128]{1,0:T(2,128)} %ghost_hbm.1) | copy-start | bytes 3076
  2.7 10.5 %collective-permute-start.1 = (f32[8,256]{1,0:T(8,128)S(1)}, f32[8,256]{1,0:T(8,128)S(1)}, u32[]{:S(2)}, u32[]{:S(2)}) collective-permute-start(f32[8,256]{1,0:T(8,128)S(1)} %pack.1.own_ref.packet_ref), channel_id=1, source_target_pairs={{0,1},{1,0},{2,3},{3,2},{4,5},{5,4},{6,7},{7,6},{8,9},{9,8},{10,11... | collective-permute-start | bytes 24584 | tf_op jit(solution)/shard_map/ppermute | solution.py:527
  6.1 7.2 %collective-permute-start = (f32[8,256]{1,0:T(8,128)S(1)}, f32[8,256]{1,0:T(8,128)S(1)}, u32[]{:S(2)}, u32[]{:S(2)}) collective-permute-start(f32[8,256]{1,0:T(8,128)S(1)} %pack.1.own_ref.packet_ref), channel_id=1, source_target_pairs={{0,15},{1,2},{2,1},{3,4},{4,3},{5,6},{6,5},{7,8},{8,7},{9,10},{10,... | collective-permute-start | bytes 24584 | tf_op jit(solution)/shard_map/ppermute | solution.py:526
  11.2 0.9 %copy-start.1 = (f32[64,512]{1,0:T(8,128)S(1)}, f32[64,512]{1,0:T(8,128)}, u32[]{:S(2)}) copy-start(f32[64,512]{1,0:T(8,128)} %sparse_ref.1) | copy-start | bytes 393220
  12.1 0.7 %copy-start.5 = (f32[2,512]{1,0:T(2,128)S(1)}, f32[2,512]{1,0:T(2,128)}, u32[]{:S(2)}) copy-start(f32[2,512]{1,0:T(2,128)} %coef_ref.1) | copy-start | bytes 12292
  13.2 0.9 %copy-start = (s32[128,256]{1,0:T(8,128)S(1)}, s32[128,256]{1,0:T(8,128)}, u32[]{:S(2)}) copy-start(s32[128,256]{1,0:T(8,128)} %nbr_ref.1) | copy-start | bytes 393220
  20.0 15.0 %collective-permute-start.2 = (f32[8,128]{1,0:T(8,128)S(1)}, f32[8,128]{1,0:T(8,128)S(1)}, u32[]{:S(2)}, u32[]{:S(2)}) collective-permute-start(f32[8,128]{1,0:T(8,128)S(1)} %get-tuple-element.15), channel_id=1, source_target_pairs={{0,15},{1,2},{2,1},{3,4},{4,3},{5,6},{6,5},{7,8},{8,7},{9,10},{10,... | collective-permute-start | bytes 12296 | tf_op jit(solution)/shard_map/ppermute | solution.py:533
  25.1 10.0 %collective-permute-start.3 = (f32[8,128]{1,0:T(8,128)S(1)}, f32[8,128]{1,0:T(8,128)S(1)}, u32[]{:S(2)}, u32[]{:S(2)}) collective-permute-start(f32[8,128]{1,0:T(8,128)S(1)} %get-tuple-element.16), channel_id=1, source_target_pairs={{0,1},{1,0},{2,3},{3,2},{4,5},{5,4},{6,7},{7,6},{8,9},{9,8},{10,11... | collective-permute-start | bytes 12296 | tf_op jit(solution)/shard_map/ppermute | solution.py:534
  30.7 0.7 %copy-start.2 = (f32[2,6,256]{2,0,1:T(2,128)S(1)}, f32[2,6,256]{2,0,1:T(2,128)}, u32[]{:S(2)}) copy-start(f32[2,6,256]{2,0,1:T(2,128)} %param.16) | copy-start | bytes 36868
  31.4 0.7 %copy-start.3 = (f32[2,3,256]{2,0,1:T(2,128)S(1)}, f32[2,3,256]{2,0,1:T(2,128)}, u32[]{:S(2)}) copy-start(f32[2,3,256]{2,0,1:T(2,128)} %param.10) | copy-start | bytes 18436

commit v2 on v1

--- a/solution.py
+++ b/solution.py
@@ -80,25 +80,37 @@
     return jnp.concatenate([p[:, 0:128] for p in pieces] + [p[:, 128:256] for p in pieces], axis=0)
 
 
-def fetch_all(sources, targets, semaphores):
+def fetch(sources, targets, semaphores):
     copies = [
         pltpu.make_async_copy(source, target, semaphores.at[i])
         for i, (source, target) in enumerate(zip(sources, targets))
     ]
     for copy in copies:
         copy.start()
-    for copy in copies:
-        copy.wait()
-
-
-def pack_kernel(positions_hbm, species_hbm, ghost_hbm, out_ref, positions, species, ghost, sems):
-    fetch_all((positions_hbm, species_hbm, ghost_hbm), (positions, species, ghost), sems)
-    out_ref[...] = jnp.concatenate(
-        [positions[c] for c in range(3)]
-        + [species[...].astype(F32)]
-        + [jnp.concatenate([ghost[0:1, :], ghost[1:2, :]], axis=1).astype(F32)],
+    return copies
+
+
+def pack_kernel(positions_ref, species_ref, ghost_ref, nbr_ref, own_ref, far_ref, near_ref):
+    rows = jnp.concatenate(
+        [positions_ref[c] for c in range(3)]
+        + [species_ref[...].astype(F32)]
+        + [jnp.concatenate([ghost_ref[0:1, :], ghost_ref[1:2, :]], axis=1).astype(F32)],
         axis=0,
     )
+    odd = odd_slab()
+    low, high = (lanes(ghost_ref[h : h + 1, :]) for h in range(2))
+    picks = jnp.where(odd, high, low), jnp.where(odd, low, high)
+    for half in range(2):
+        block = slice(half * 8, half * 8 + 8)
+        part = rows[:, half * 128 : half * 128 + 128]
+        own_ref[block, :] = part
+        far_ref[block, :] = part
+        near_ref[block, :] = part
+    for s in range(16):
+        block = slice(s * 8, s * 8 + 8)
+        left, right = nbr_ref[block, 0:128], nbr_ref[block, 128:256]
+        for target, pick in zip((far_ref, near_ref), picks):
+            target[16 + s * 8 : 24 + s * 8, :] = take_pair(left, right, pick).astype(F32)
 
 
 def split(value):
@@ -141,13 +153,23 @@
     return jnp.exp(away * away * -0.5)
 
 
-def quad_kernel(sparse_ref, coef_ref, quad_ref):
-    sparse = sparse_ref[...]
+def quadratic(sparse, weight):
     basis = sparse * lax.rsqrt(jnp.sum(sparse * sparse, axis=0, keepdims=True) + 1e-6)
-    scaled = jnp.concatenate([basis * coef_ref[0:1, :], basis * coef_ref[1:2, :]], axis=0)
-    quad_ref[...] = lax.dot_general(
+    scaled = jnp.concatenate([basis * weight[0:1], basis * weight[1:2]], axis=0)
+    return lax.dot_general(
         scaled, basis, (((1,), (1,)), ((), ())), precision=HI, preferred_element_type=F32
     )
+
+
+def places(own):
+    same = lax.broadcasted_iota(jnp.int32, (256, 256), 0) == own[7:8].astype(jnp.int32)
+    place = lax.broadcasted_iota(jnp.int32, (8, 256), 1).astype(F32).astype(BF16)
+    return lax.dot_general(
+        place,
+        jnp.where(same, 1.0, 0.0).astype(BF16),
+        (((1,), (1,)), ((), ())),
+        preferred_element_type=F32,
+    ).astype(jnp.int32)
 
 
 def scatter(slots, hot_of, value_of):
@@ -191,74 +213,38 @@
 
 
 def joined(sums):
-    grad = jnp.concatenate([sums[0:8] + sums[8:16], sums[16:24] + sums[24:32]], axis=1)
+    grad = jnp.concatenate(
+        [sums[c : c + 8] + sums[c + 8 : c + 16] for c in range(0, sums.shape[0], 16)], axis=1
+    )
     return jnp.where(lax.broadcasted_iota(jnp.int32, grad.shape, 0) < 6, grad, 0.0)
 
 
-def force_kernel(
-    own_ref,
-    far_ref,
-    close_ref,
-    nbr_ref,
-    quad_ref,
-    to_far_ref,
-    to_near_ref,
-    grad_ref,
-    v_ref,
-    index_ref,
-    central_ref,
-    low_ref,
-    code_ref,
-    src_ref,
-    hyd_ref,
-    t_ref,
-    geo_ref,
-    e_ref,
-    p_ref,
-    desc_ref,
-    g_ref,
-):
-    odd = odd_slab()
-
-    far = far_ref[...]
-    close = close_ref[...]
-    far_low, far_high = (lanes(far[7:8, h * 128 : h * 128 + 128]) for h in range(2))
-    close_low, close_high = (lanes(close[7:8, h * 128 : h * 128 + 128]) for h in range(2))
-    far_pick = jnp.where(odd, far_low, far_high).astype(jnp.int32)
-    close_pick = jnp.where(odd, close_high, close_low).astype(jnp.int32)
-    far = take_pair(far[:, 0:128], far[:, 128:256], far_pick)
-    close = take_pair(close[:, 0:128], close[:, 128:256], close_pick)
-    own = own_ref[...]
-    listed = own[7:8].astype(jnp.int32)
-    chunks = [
-        own[:, 0:128],
-        own[:, 128:256],
-        jnp.where(odd, close, far),
-        jnp.where(odd, far, close),
-    ]
-    for c in range(4):
-        for r in range(7):
-            src_ref[c * 7 + r] = lanes(chunks[c][r : r + 1])
+def pair_forces(chunks, picks, index_of, code_of, quad_of, grad_ref, work):
+    (v_ref, central_ref, low_ref, code_ref, src_ref, hyd_ref, t_ref, geo_ref, e_ref, p_ref) = work[:10]
+    desc_ref, g_ref = work[10:]
+    for half in range(2):
+        for c in range(3):
+            for r in range(7):
+                src_ref[(half * 3 + c) * 7 + r] = lanes(chunks[half][c][r : r + 1])
 
     for half in range(2):
         cols = slice(half * 128, half * 128 + 128)
-        pick = lanes(listed[:, cols])
-        central_ref[:, cols] = take_pair(chunks[0], chunks[1], pick)
-
-        def gather(s, carry, half=half, cols=cols, pick=pick):
+        central_ref[:, cols] = take_pair(chunks[half][0], chunks[half][1], picks[half])
+
+        def gather(s, carry, half=half, cols=cols):
             rows = pl.ds(pl.multiple_of(s * 8, 8), 8)
-            index = take_pair(nbr_ref[rows, 0:128], nbr_ref[rows, 128:256], pick)
-            index_ref[half, rows, :] = index
+            index = index_of(half, rows)
             local = index & 127
             first = index < 128
             own = index < 256
             live = index < 512
-            low_ref[half, rows, :] = (index & 63).astype(F32)
-            code_ref[half, rows, :] = jnp.where(live & ~own, local >> 6, 2).astype(F32)
+            low, code = code_of(index)
+            low_ref[half, rows, :] = low.astype(F32)
+            code_ref[half, rows, :] = code.astype(F32)
 
             def fetch(r):
-                mine = jnp.where(first, take(src_ref[r], local), take(src_ref[7 + r], local))
-                return jnp.where(own, mine, take(src_ref[14 + half * 7 + r], local))
+                found = [take(src_ref[(half * 3 + c) * 7 + r], local) for c in range(3)]
+                return jnp.where(own, jnp.where(first, found[0], found[1]), found[2])
 
             hyd_ref[half, rows, :] = fetch(6)
             for b in range(2):
@@ -323,7 +309,7 @@
     desc = [desc_ref[bl] for bl in range(4)]
     norm = [lax.rsqrt(jnp.sum(d * d, axis=0, keepdims=True) + 1e-6) for d in desc]
     unit = [d * n for d, n in zip(desc, norm)]
-    turned = dot3(quad_ref[...], jnp.concatenate(unit, axis=1))
+    turned = dot3(quad_of(), jnp.concatenate(unit, axis=1))
     tap = jnp.concatenate([taps()] * 8, axis=0)
     for bl in range(4):
         half = bl & 1
@@ -334,7 +320,8 @@
         g_ref[bl] = (2.0 * norm[bl]) * (slope - unit[bl] * along) * tap
 
     group = 4
-    grad_ref[6:8, :] = jnp.zeros((2, 256), F32)
+    if grad_ref is not None:
+        grad_ref[6:8, :] = jnp.zeros((2, 256), F32)
     for b in range(2):
         for half in range(2):
             bl = b * 2 + half
@@ -370,30 +357,155 @@
             zero = jnp.zeros((8, 128), F32)
             total = lax.fori_loop(0, 16 // group, back, (zero,) * 3, unroll=4)
             for c in range(3):
-                grad_ref[c * 2 + b : c * 2 + b + 1, half * 128 : half * 128 + 128] = -jnp.sum(
-                    total[c], axis=0, keepdims=True
-                )
-
-    copies = []
+                if grad_ref is not None:
+                    grad_ref[c * 2 + b : c * 2 + b + 1, half * 128 : half * 128 + 128] = -jnp.sum(
+                        total[c], axis=0, keepdims=True
+                    )
+
+
+def merged_kernel(
+    own_hbm,
+    far_hbm,
+    near_hbm,
+    nbr_hbm,
+    sparse_hbm,
+    coef_hbm,
+    momenta_hbm,
+    noise_hbm,
+    tables_hbm,
+    forces_ref,
+    send_ref,
+    own_ref,
+    far_ref,
+    near_ref,
+    nbr_ref,
+    sparse_ref,
+    coef_ref,
+    momenta_ref,
+    noise_ref,
+    table_ref,
+    sems,
+    quad_ref,
+    grad_ref,
+    *work,
+):
+    copies = fetch(
+        (own_hbm, far_hbm, near_hbm, nbr_hbm, sparse_hbm, coef_hbm, momenta_hbm, noise_hbm)
+        + (tables_hbm.at[lax.axis_index("bead")],),
+        (own_ref, far_ref, near_ref, nbr_ref, sparse_ref, coef_ref, momenta_ref, noise_ref)
+        + (table_ref,),
+        sems,
+    )
+    for copy in copies[:4]:
+        copy.wait()
+    odd = odd_slab()
+    chunk = lambda ref, h: ref[h * 8 : h * 8 + 8, :]
+    own = [chunk(own_ref, h) for h in range(2)]
+    far = [chunk(far_ref, h) for h in range(2)]
+    near = [chunk(near_ref, h) for h in range(2)]
+    below = [jnp.where(odd, n, f) for f, n in zip(far, near)]
+    above = [jnp.where(odd, f, n) for f, n in zip(far, near)]
+    listed = lambda slab, h: lanes(slab[h][7:8]).astype(jnp.int32)
+
+    def quad_of():
+        for copy in copies[4:]:
+            copy.wait()
+        quad_ref[...] = quadratic(sparse_ref[...], coef_ref[...])
+        return quad_ref[...]
+
+    mine = [listed(own, h) for h in range(2)]
+    outer = [listed(below, 1), listed(above, 0)]
+    copied = [take_pair(*below, outer[0]), take_pair(*above, outer[1])]
+    pair_forces(
+        [(*own, copied[h]) for h in range(2)],
+        mine,
+        lambda half, rows: take_pair(nbr_ref[rows, 0:128], nbr_ref[rows, 128:256], mine[half]),
+        lambda index: (index & 63, index >> 6),
+        quad_of,
+        grad_ref,
+        work,
+    )
+    v_ref, _, low_ref, code_ref = work[:4]
+    level = levels(64, 256)
+    wide = lambda ref, rows: jnp.concatenate([ref[h, rows, :] for h in range(2)], axis=1)
+    passed = joined(
+        scatter(
+            128,
+            lambda slot: one_hot(wide(low_ref, pl.ds(slot, 1)), level),
+            lambda slot: coded(wide(v_ref, pl.ds(slot * 8, 8)), wide(code_ref, pl.ds(slot, 1)), 4),
+        )
+    )
+
+    def index_of(half, rows):
+        there = pl.ds(16 + rows.start, rows.size)
+        f, n = far_ref[there, :], near_ref[there, :]
+        found = jnp.where(odd, n, f) if half == 0 else jnp.where(odd, f, n)
+        return found.astype(jnp.int32)
+
+    def code_of(index):
+        own = (index >= 256) & (index < 512)
+        return index & 63, jnp.where(own, (index & 127) >> 6, 2)
+
+    pair_forces(
+        [
+            (*slab, take_pair(*own, pick))
+            for slab, pick in ((below, mine[0]), (above, mine[1]))
+        ],
+        outer,
+        index_of,
+        code_of,
+        lambda: quad_ref[...],
+        None,
+        work,
+    )
     level = levels(64, 128)
-    for half in range(2):
-        sums = scatter(
-            128,
-            lambda slot, half=half: one_hot(low_ref[half, pl.ds(slot, 1), :], level),
-            lambda slot, half=half: coded(
-                v_ref[half, pl.ds(slot * 8, 8), :],
-                code_ref[half, pl.ds(slot, 1), :],
-                2,
-            ),
+    returned = [
+        joined(
+            scatter(
+                128,
+                lambda slot, half=half: one_hot(low_ref[half, pl.ds(slot, 1), :], level),
+                lambda slot, half=half: coded(
+                    v_ref[half, pl.ds(slot * 8, 8), :], code_ref[half, pl.ds(slot, 1), :], 2
+                ),
+            )
         )
-        copies.append(joined(sums))
-    to_far_ref[...] = jnp.where(odd, copies[1], copies[0])
-    to_near_ref[...] = jnp.where(odd, copies[0], copies[1])
-
-
-def push_rows(grad, packet_ref):
+        for half in range(2)
+    ]
+    own = jnp.concatenate(own, axis=1)
+    back = places(own)
+    total = grad_ref[...] + jnp.concatenate(returned, axis=1)
+    grad = passed + jnp.concatenate(
+        [
+            take_pair(total[:, 0:128], total[:, 128:256], back[:, h * 128 : h * 128 + 128])
+            for h in range(2)
+        ],
+        axis=1,
+    )
+    for c in range(3):
+        forces_ref[c] = -grad[c * 2 : c * 2 + 2]
+    rows = base_rows(own, momenta_ref, noise_ref) + push_rows(grad, own)
+    send_ref[...] = jnp.dot(table_ref[...], rows, precision=HI, preferred_element_type=F32)
+
+
+WORK = [
+    (2, 1024, 128),
+    (8, 256),
+    (2, 128, 128),
+    (2, 128, 128),
+    (42, 8, 128),
+    (2, 128, 128),
+    (4, 128, 128),
+    (4, 5, 128, 128),
+    (4, 2, 128, 128),
+    (4, 32, 128, 128),
+    (4, 64, 128),
+    (4, 64, 128),
+]
+
+
+def push_rows(grad, own):
     push = grad * -0.25
-    mass = jnp.where(packet_ref[6:7, :] > 0.5, 1.0, 16.0)
+    mass = jnp.where(own[6:7] > 0.5, 1.0, 16.0)
     none = jnp.zeros((8, 256), F32)
     return halves([none, none, push / mass, push, none, none, none])
 
@@ -411,77 +523,6 @@
     )
 
 
-def places(packet_ref):
-    listed = packet_ref[7:8, :].astype(jnp.int32)
-    same = lax.broadcasted_iota(jnp.int32, (256, 256), 0) == listed
-    place = lax.broadcasted_iota(jnp.int32, (8, 256), 1).astype(F32).astype(BF16)
-    return lax.dot_general(
-        place,
-        jnp.where(same, 1.0, 0.0).astype(BF16),
-        (((1,), (1,)), ((), ())),
-        preferred_element_type=F32,
-    ).astype(jnp.int32)
-
-
-def gather_kernel(
-    v_ref,
-    index_ref,
-    grad_ref,
-    packet_ref,
-    momenta_ref,
-    noise_ref,
-    table_ref,
-    own_ref,
-    sum_ref,
-    back_ref,
-):
-    back_ref[...] = places(packet_ref)
-    level = levels(128, 256)
-    wide = lambda pick, slot: jnp.concatenate([pick(h, slot) for h in range(2)], axis=1)
-    index = lambda slot: wide(lambda h, s: index_ref[h, pl.ds(s, 1), :], slot)
-    sums = scatter(
-        128,
-        lambda slot: one_hot((index(slot) & 127).astype(F32), level),
-        lambda slot: coded(
-            wide(lambda h, s: v_ref[h, pl.ds(s * 8, 8), :], slot),
-            (index(slot) >> 7).astype(F32),
-            2,
-        ),
-    )
-    passed = joined(sums)
-    central = jnp.concatenate(
-        [
-            take_pair(grad_ref[:, 0:128], grad_ref[:, 128:256], back_ref[:, 0:128]),
-            take_pair(grad_ref[:, 0:128], grad_ref[:, 128:256], back_ref[:, 128:256]),
-        ],
-        axis=1,
-    )
-    own = passed + central
-    own_ref[...] = own
-    sum_ref[...] = jnp.dot(
-        table_ref[...],
-        base_rows(packet_ref[...], momenta_ref, noise_ref) + push_rows(own, packet_ref),
-        precision=HI,
-        preferred_element_type=F32,
-    )
-
-
-def combine_kernel(
-    far_ref, near_ref, back_ref, packet_ref, table_ref, own_ref, base_ref, forces_ref, send_ref
-):
-    odd = odd_slab()
-    low = jnp.where(odd, near_ref[...], far_ref[...])
-    high = jnp.where(odd, far_ref[...], near_ref[...])
-    passed = jnp.concatenate(
-        [take_pair(low, high, back_ref[:, 0:128]), take_pair(low, high, back_ref[:, 128:256])],
-        axis=1,
-    )
-    forces = -own_ref[...] - passed
-    for c in range(3):
-        forces_ref[c] = forces[c * 2 : c * 2 + 2]
-    send_ref[...] = base_ref[...] + dot3(table_ref[...], push_rows(passed, packet_ref))
-
-
 def finish_kernel(parts_ref, positions_ref, momenta_ref):
     total = parts_ref[0]
     for d in range(1, 16):
@@ -494,23 +535,25 @@
             momenta_ref[c, :, cols] = total[row + 6 : row + 8]
 
 
-def call(kernel, shapes, count, name, mib=1, scratch=(), ints=(), fetched=()):
-    buffers = [pltpu.VMEM(shape, F32) for shape in scratch]
-    buffers += [pltpu.VMEM(value.shape, value.dtype) for value in fetched]
+LIMIT = 62
+
+
+def call(kernel, shapes, operands, name, mib, fetched=(), scratch=()):
+    buffers = [
+        pltpu.VMEM(value.shape[1:] if value.shape == STEP_TABLE.shape else value.shape, value.dtype)
+        for value in fetched
+    ]
     if fetched:
         buffers.append(pltpu.SemaphoreType.DMA((len(fetched),)))
     return pl.pallas_call(
         kernel,
-        out_shape=[
-            jax.ShapeDtypeStruct(shape, jnp.int32 if i in ints else F32)
-            for i, shape in enumerate(shapes)
-        ],
-        in_specs=[WHOLE] * count + [pl.BlockSpec(memory_space=pltpu.HBM)] * len(fetched),
+        out_shape=[jax.ShapeDtypeStruct(shape, F32) for shape in shapes],
+        in_specs=[WHOLE] * len(operands) + [pl.BlockSpec(memory_space=pl.ANY)] * len(fetched),
         out_specs=[WHOLE] * len(shapes),
-        scratch_shapes=buffers,
+        scratch_shapes=buffers + [pltpu.VMEM(shape, F32) for shape in scratch],
         compiler_params=pltpu.CompilerParams(vmem_limit_bytes=mib * 1024 * 1024),
         name=name,
-    )
+    )(*operands, *fetched)
 
 
 def per_device(
@@ -520,51 +563,28 @@
     close = [(i, i ^ 1) for i in range(size)]
     distant = [(i, (i + 1) % size if i % 2 else (i - 1) % size) for i in range(size)]
     turn = lambda value: jnp.transpose(value, (1, 0, 2))
-    kind = species.reshape(1, 256)
-    own = (turn(positions), kind, ghost_index)
-    (packet,) = call(pack_kernel, [(8, 256)], 0, "pack", fetched=own)(*own)
-    far = lax.ppermute(packet, "space", distant)
-    near = lax.ppermute(packet, "space", close)
-    table = lax.dynamic_index_in_dim(
-        jnp.asarray(STEP_TABLE), lax.axis_index("bead"), 0, keepdims=False
-    )
-    (quad,) = call(quad_kernel, [(128, 64)], 2, "quad", 2)(sparse_points, coefficients)
-    to_far, to_near, grad, pulls, index = table_gradient(packet, far, near, neighbours, quad)
-    from_far = lax.ppermute(to_far, "space", distant)
-    from_near = lax.ppermute(to_near, "space", close)
-    own_grad, summed, back = call(
-        gather_kernel, [(8, 256), (384, 128), (8, 256)], 7, "gather", 8, ints=(2,)
-    )(pulls, index, grad, packet, turn(momenta), turn(noise), table)
-    forces, send = call(combine_kernel, [(3, 2, 256), (384, 128)], 7, "combine", 4)(
-        from_far, from_near, back, packet, table, own_grad, summed
+    own, to_far, to_near = call(
+        pack_kernel,
+        [(16, 128), (144, 128), (144, 128)],
+        (turn(positions), species.reshape(1, 256), ghost_index, neighbours),
+        "pack",
+        LIMIT,
+    )
+    far = lax.ppermute(to_far, "space", distant)
+    near = lax.ppermute(to_near, "space", close)
+    forces, send = call(
+        merged_kernel,
+        [(3, 2, 256), (384, 128)],
+        (),
+        "forces",
+        LIMIT,
+        (own, far, near, neighbours, sparse_points, coefficients, turn(momenta), turn(noise))
+        + (jnp.asarray(STEP_TABLE),),
+        [(128, 64), (8, 256)] + WORK,
     )
     parts = lax.all_to_all(send.reshape(16, 24, 128), "bead", split_axis=0, concat_axis=0, tiled=True)
-    new_positions, new_momenta = call(finish_kernel, [(3, 2, 256)] * 2, 1, "finish")(parts)
+    new_positions, new_momenta = call(finish_kernel, [(3, 2, 256)] * 2, (parts,), "finish", 1)
     return (turn(new_positions), turn(new_momenta), turn(forces))
-
-
-def table_gradient(*args):
-    return call(
-        force_kernel,
-        [(8, 128), (8, 128), (8, 256), (2, 1024, 128), (2, 128, 128)],
-        5,
-        "force",
-        20,
-        scratch=[
-            (8, 256),
-            (2, 128, 128),
-            (2, 128, 128),
-            (28, 8, 128),
-            (2, 128, 128),
-            (4, 128, 128),
-            (4, 5, 128, 128),
-            (4, 2, 128, 128),
-            (4, 32, 128, 128),
-            (4, 64, 128),
-            (4, 64, 128),
-        ],
-        ints=(4,),
-    )(*args)
 
 
 def solution(mesh):

time: 51.4 us -> 47.8 us (0.930)
  the two profiles are of different devices: /device:TPU:1 before, /device:TPU:8 now
where the time goes in v2:
time: 47.8 us; the launch traced here: 47.5 us
  Pallas kernels  18.1 us (38%)
  blocking collectives  16.9 us (35%)
  starting transfers between devices  8.83 us (18%)
  waiting for transfers between devices  2.35 us (5%)
  local copies, waits for them, and re-layouts  0.67 us (1%)
  between operations  0.64 us (1%)
    pallas_call x3, Pallas kernels, call(): pl.pallas_call(kernel, out_shape=[jax.ShapeDtypeStruct(shape, F32) for sh...  18.1 us
    all_to_all x1, blocking collectives, per_device(): lax.all_to_all(send.reshape(16, 24, 128), 'bead', split_axis=0, concat_ax...  16.9 us
    ppermute x1, starting transfers between devices, per_device(): far = lax.ppermute(to_far, 'space', distant)  8.82 us
    ppermute x1, waiting for transfers between devices, per_device(): far = lax.ppermute(to_far, 'space', distant)  2.35 us
  transfers between devices with their start and end apart: 2, of which 1 were waited for; matrix products, arithmetic and copies ran while one was open for 0% of the time, Pallas kernels for 0%

profile of v2, /device:TPU:8, one launch (start us, length us, event | category | flops | bytes accessed | tf_op | source)
XLA Modules:
  0.0 47.5 jit_solution(1422527410103866628)
XLA Ops:
  0.6 1.8 %pack.1 = (f32[16,128]{1,0:T(8,128)}, f32[144,128]{1,0:T(8,128)}, f32[144,128]{1,0:T(8,128)}) custom-call(f32[3,2,256]{2,1,0:T(2,128)} %bitcast.10, s32[1,256]{1,0:T(1,128)} %bitcast.12, s32[2,128]{1,0:T(2,128)} %ghost_ref.1, s32[128,256]{1,0:T(8,128)} %nbr_hbm.1), custom_call_target="tpu_custom_call" | custom-call | tf_op jit(solution)/shard_map/pack/pallas_call | solution.py:548
  2.5 8.8 %collective-permute-start = (f32[144,128]{1,0:T(8,128)}, f32[144,128]{1,0:T(8,128)S(1)}, u32[]{:S(2)}, u32[]{:S(2)}) collective-permute-start(f32[144,128]{1,0:T(8,128)} %get-tuple-element.11), channel_id=1, source_target_pairs={{0,15},{1,2},{2,1},{3,4},{4,3},{5,6},{6,5},{7,8},{8,7},{9,10},{10,... | collective-permute-start | bytes 221192 | tf_op jit(solution)/shard_map/ppermute | solution.py:573
  11.3 0.0 collective-permute-start.1
  11.3 2.3 %collective-permute-done.far_hbm = f32[144,128]{1,0:T(8,128)S(1)} collective-permute-done((f32[144,128]{1,0:T(8,128)}, f32[144,128]{1,0:T(8,128)S(1)}, u32[]{:S(2)}, u32[]{:S(2)}) %collective-permute-start) | collective-permute-done | bytes 73760 | tf_op jit(solution)/shard_map/ppermute | solution.py:573
  13.6 0.0 copy-start
  13.6 0.0 collective-permute-done.1.near_hbm
  13.6 0.0 copy-start.1
  13.6 0.6 %copy-done = f32[144,128]{1,0:T(8,128)} copy-done((f32[144,128]{1,0:T(8,128)}, f32[144,128]{1,0:T(8,128)S(1)}, u32[]{:S(2)}) %copy-start) | copy-done | bytes 73752
  14.3 0.0 copy-done.1
  14.3 15.7 %forces.1 = (f32[3,2,256]{2,1,0:T(2,128)}, f32[384,128]{1,0:T(8,128)}) custom-call(f32[16,128]{1,0:T(8,128)} %get-tuple-element.10.own_hbm, f32[144,128]{1,0:T(8,128)} %copy-done, f32[144,128]{1,0:T(8,128)} %copy-done.1, s32[128,256]{1,0:T(8,128)} %nbr_hbm.1, f32[64,512]{1,0:T(8,128)} %sparse_hbm.1, f32[2,512]{1,0:T(2,128)} %coef_hbm.1, ...), custom_call_target="tpu_custom_call" | custom-call | tf_op jit(solution)/shard_map/forces/pallas_call | solution.py:548
  30.0 16.9 %all_to_all.5.parts_ref = f32[16,24,128]{2,1,0:T(8,128)S(1)} all-to-all(f32[16,24,128]{2,1,0:T(8,128)} %bitcast.8), channel_id=1, replica_groups=mesh['bead'=16,'space'=16] {'bead'}, dimensions={0} | all-to-all | bytes 393216 | tf_op jit(solution)/shard_map/all_to_all | solution.py:585
  46.9 0.6 %finish.1 = (f32[3,2,256]{2,1,0:T(2,128)}, f32[3,2,256]{2,1,0:T(2,128)}) custom-call(f32[16,24,128]{2,1,0:T(8,128)S(1)} %all_to_all.5.parts_ref), custom_call_target="tpu_custom_call" | custom-call | tf_op jit(solution)/shard_map/finish/pallas_call | solution.py:548
Async XLA Ops:
  2.5 11.2 %collective-permute-start = (f32[144,128]{1,0:T(8,128)}, f32[144,128]{1,0:T(8,128)S(1)}, u32[]{:S(2)}, u32[]{:S(2)}) collective-permute-start(f32[144,128]{1,0:T(8,128)} %get-tuple-element.11), channel_id=1, source_target_pairs={{0,15},{1,2},{2,1},{3,4},{4,3},{5,6},{6,5},{7,8},{8,7},{9,10},{10,... | collective-permute-start | bytes 221192 | tf_op jit(solution)/shard_map/ppermute | solution.py:573
  11.3 2.4 %collective-permute-start.1 = (f32[144,128]{1,0:T(8,128)}, f32[144,128]{1,0:T(8,128)S(1)}, u32[]{:S(2)}, u32[]{:S(2)}) collective-permute-start(f32[144,128]{1,0:T(8,128)} %get-tuple-element.12), channel_id=1, source_target_pairs={{0,1},{1,0},{2,3},{3,2},{4,5},{5,4},{6,7},{7,6},{8,9},{9,8},{10,11... | collective-permute-start | bytes 221192 | tf_op jit(solution)/shard_map/ppermute | solution.py:574
  13.6 0.6 %copy-start = (f32[144,128]{1,0:T(8,128)}, f32[144,128]{1,0:T(8,128)S(1)}, u32[]{:S(2)}) copy-start(f32[144,128]{1,0:T(8,128)S(1)} %collective-permute-done.far_hbm) | copy-start | bytes 221188
  13.6 0.7 %copy-start.1 = (f32[144,128]{1,0:T(8,128)}, f32[144,128]{1,0:T(8,128)S(1)}, u32[]{:S(2)}) copy-start(f32[144,128]{1,0:T(8,128)S(1)} %collective-permute-done.1.near_hbm) | copy-start | bytes 221188

commit v3 on v2

--- a/solution.py
+++ b/solution.py
@@ -269,6 +269,7 @@
 
         lax.fori_loop(0, 16, gather, 0, unroll=16)
 
+    yield
     tap = taps()
 
     def radial(bl, carry):
@@ -306,6 +307,7 @@
 
     lax.fori_loop(0, 4, radial, 0, unroll=4)
 
+    yield
     desc = [desc_ref[bl] for bl in range(4)]
     norm = [lax.rsqrt(jnp.sum(d * d, axis=0, keepdims=True) + 1e-6) for d in desc]
     unit = [d * n for d, n in zip(desc, norm)]
@@ -319,6 +321,7 @@
         along = jnp.sum(slope * unit[bl], axis=0, keepdims=True)
         g_ref[bl] = (2.0 * norm[bl]) * (slope - unit[bl] * along) * tap
 
+    yield
     group = 4
     if grad_ref is not None:
         grad_ref[6:8, :] = jnp.zeros((2, 256), F32)
@@ -389,6 +392,7 @@
     grad_ref,
     *work,
 ):
+    work, outer_work = work[: len(WORK)], work[len(WORK) :]
     copies = fetch(
         (own_hbm, far_hbm, near_hbm, nbr_hbm, sparse_hbm, coef_hbm, momenta_hbm, noise_hbm)
         + (tables_hbm.at[lax.axis_index("bead")],),
@@ -416,7 +420,7 @@
     mine = [listed(own, h) for h in range(2)]
     outer = [listed(below, 1), listed(above, 0)]
     copied = [take_pair(*below, outer[0]), take_pair(*above, outer[1])]
-    pair_forces(
+    inner_pairs = pair_forces(
         [(*own, copied[h]) for h in range(2)],
         mine,
         lambda half, rows: take_pair(nbr_ref[rows, 0:128], nbr_ref[rows, 128:256], mine[half]),
@@ -425,6 +429,31 @@
         grad_ref,
         work,
     )
+    def index_of(half, rows):
+        there = pl.ds(16 + rows.start, rows.size)
+        f, n = far_ref[there, :], near_ref[there, :]
+        found = jnp.where(odd, n, f) if half == 0 else jnp.where(odd, f, n)
+        return found.astype(jnp.int32)
+
+    def code_of(index):
+        own = (index >= 256) & (index < 512)
+        return index & 63, jnp.where(own, (index & 127) >> 6, 2)
+
+    outer_pairs = pair_forces(
+        [
+            (*slab, take_pair(*own, pick))
+            for slab, pick in ((below, mine[0]), (above, mine[1]))
+        ],
+        outer,
+        index_of,
+        code_of,
+        lambda: quad_ref[...],
+        None,
+        outer_work,
+    )
+    for pairs in (inner_pairs, outer_pairs):
+        for _ in range(4):
+            next(pairs, None)
     v_ref, _, low_ref, code_ref = work[:4]
     level = levels(64, 256)
     wide = lambda ref, rows: jnp.concatenate([ref[h, rows, :] for h in range(2)], axis=1)
@@ -436,28 +465,7 @@
         )
     )
 
-    def index_of(half, rows):
-        there = pl.ds(16 + rows.start, rows.size)
-        f, n = far_ref[there, :], near_ref[there, :]
-        found = jnp.where(odd, n, f) if half == 0 else jnp.where(odd, f, n)
-        return found.astype(jnp.int32)
-
-    def code_of(index):
-        own = (index >= 256) & (index < 512)
-        return index & 63, jnp.where(own, (index & 127) >> 6, 2)
-
-    pair_forces(
-        [
-            (*slab, take_pair(*own, pick))
-            for slab, pick in ((below, mine[0]), (above, mine[1]))
-        ],
-        outer,
-        index_of,
-        code_of,
-        lambda: quad_ref[...],
-        None,
-        work,
-    )
+    v_ref, _, low_ref, code_ref = outer_work[:4]
     level = levels(64, 128)
     returned = [
         joined(
@@ -484,7 +492,7 @@
     for c in range(3):
         forces_ref[c] = -grad[c * 2 : c * 2 + 2]
     rows = base_rows(own, momenta_ref, noise_ref) + push_rows(grad, own)
-    send_ref[...] = jnp.dot(table_ref[...], rows, precision=HI, preferred_element_type=F32)
+    send_ref[...] = dot3(table_ref[...], rows)
 
 
 WORK = [
@@ -580,7 +588,7 @@
         LIMIT,
         (own, far, near, neighbours, sparse_points, coefficients, turn(momenta), turn(noise))
         + (jnp.asarray(STEP_TABLE),),
-        [(128, 64), (8, 256)] + WORK,
+        [(128, 64), (8, 256)] + WORK + WORK,
     )
     parts = lax.all_to_all(send.reshape(16, 24, 128), "bead", split_axis=0, concat_axis=0, tiled=True)
     new_positions, new_momenta = call(finish_kernel, [(3, 2, 256)] * 2, (parts,), "finish", 1)

time: 47.8 us -> 45.2 us (0.946)
  Pallas kernels: 18.1 us -> 15.6 us
    pallas_call x3, Pallas kernels: 18.1 us -> 15.6 us  [call(): pl.pallas_call(kernel, out_shape=[jax.ShapeDtypeStruct(shape, F32) for sh...]
where the time goes in v3:
time: 45.2 us; the launch traced here: 45 us
  blocking collectives  16.9 us (37%)
  Pallas kernels  15.6 us (35%)
  starting transfers between devices  8.83 us (20%)
  waiting for transfers between devices  2.35 us (5%)
  local copies, waits for them, and re-layouts  0.67 us (1%)
  between operations  0.64 us (1%)
    all_to_all x1, blocking collectives, per_device(): lax.all_to_all(send.reshape(16, 24, 128), 'bead', split_axis=0, concat_ax...  16.9 us
    pallas_call x3, Pallas kernels, call(): pl.pallas_call(kernel, out_shape=[jax.ShapeDtypeStruct(shape, F32) for sh...  15.6 us
    ppermute x1, starting transfers between devices, per_device(): far = lax.ppermute(to_far, 'space', distant)  8.82 us
    ppermute x1, waiting for transfers between devices, per_device(): far = lax.ppermute(to_far, 'space', distant)  2.35 us
  transfers between devices with their start and end apart: 2, of which 1 were waited for; matrix products, arithmetic and copies ran while one was open for 0% of the time, Pallas kernels for 0%

profile of v3, /device:TPU:8, one launch (start us, length us, event | category | flops | bytes accessed | tf_op | source)
XLA Modules:
  0.0 45.0 jit_solution(14058892232319854113)
XLA Ops:
  0.6 1.8 %pack.1 = (f32[16,128]{1,0:T(8,128)}, f32[144,128]{1,0:T(8,128)}, f32[144,128]{1,0:T(8,128)}) custom-call(f32[3,2,256]{2,1,0:T(2,128)} %bitcast.10, s32[1,256]{1,0:T(1,128)} %bitcast.12, s32[2,128]{1,0:T(2,128)} %ghost_ref.1, s32[128,256]{1,0:T(8,128)} %nbr_hbm.1), custom_call_target="tpu_custom_call" | custom-call | tf_op jit(solution)/shard_map/pack/pallas_call | solution.py:556
  2.5 8.8 %collective-permute-start = (f32[144,128]{1,0:T(8,128)}, f32[144,128]{1,0:T(8,128)S(1)}, u32[]{:S(2)}, u32[]{:S(2)}) collective-permute-start(f32[144,128]{1,0:T(8,128)} %get-tuple-element.11), channel_id=1, source_target_pairs={{0,15},{1,2},{2,1},{3,4},{4,3},{5,6},{6,5},{7,8},{8,7},{9,10},{10,... | collective-permute-start | bytes 221192 | tf_op jit(solution)/shard_map/ppermute | solution.py:581
  11.3 0.0 collective-permute-start.1
  11.3 2.3 %collective-permute-done.far_hbm = f32[144,128]{1,0:T(8,128)S(1)} collective-permute-done((f32[144,128]{1,0:T(8,128)}, f32[144,128]{1,0:T(8,128)S(1)}, u32[]{:S(2)}, u32[]{:S(2)}) %collective-permute-start) | collective-permute-done | bytes 73760 | tf_op jit(solution)/shard_map/ppermute | solution.py:581
  13.6 0.0 copy-start
  13.6 0.0 collective-permute-done.1.near_hbm
  13.6 0.0 copy-start.1
  13.6 0.6 %copy-done = f32[144,128]{1,0:T(8,128)} copy-done((f32[144,128]{1,0:T(8,128)}, f32[144,128]{1,0:T(8,128)S(1)}, u32[]{:S(2)}) %copy-start) | copy-done | bytes 73752
  14.3 0.0 copy-done.1
  14.3 13.1 %forces.1 = (f32[3,2,256]{2,1,0:T(2,128)}, f32[384,128]{1,0:T(8,128)}) custom-call(f32[16,128]{1,0:T(8,128)} %get-tuple-element.10.own_hbm, f32[144,128]{1,0:T(8,128)} %copy-done, f32[144,128]{1,0:T(8,128)} %copy-done.1, s32[128,256]{1,0:T(8,128)} %nbr_hbm.1, f32[64,512]{1,0:T(8,128)} %sparse_hbm.1, f32[2,512]{1,0:T(2,128)} %coef_hbm.1, ...), custom_call_target="tpu_custom_call" | custom-call | tf_op jit(solution)/shard_map/forces/pallas_call | solution.py:556
  27.4 16.9 %all_to_all.5.parts_ref = f32[16,24,128]{2,1,0:T(8,128)S(1)} all-to-all(f32[16,24,128]{2,1,0:T(8,128)} %bitcast.8), channel_id=1, replica_groups=mesh['bead'=16,'space'=16] {'bead'}, dimensions={0} | all-to-all | bytes 393216 | tf_op jit(solution)/shard_map/all_to_all | solution.py:593
  44.3 0.6 %finish.1 = (f32[3,2,256]{2,1,0:T(2,128)}, f32[3,2,256]{2,1,0:T(2,128)}) custom-call(f32[16,24,128]{2,1,0:T(8,128)S(1)} %all_to_all.5.parts_ref), custom_call_target="tpu_custom_call" | custom-call | tf_op jit(solution)/shard_map/finish/pallas_call | solution.py:556
Async XLA Ops:
  2.5 11.2 %collective-permute-start = (f32[144,128]{1,0:T(8,128)}, f32[144,128]{1,0:T(8,128)S(1)}, u32[]{:S(2)}, u32[]{:S(2)}) collective-permute-start(f32[144,128]{1,0:T(8,128)} %get-tuple-element.11), channel_id=1, source_target_pairs={{0,15},{1,2},{2,1},{3,4},{4,3},{5,6},{6,5},{7,8},{8,7},{9,10},{10,... | collective-permute-start | bytes 221192 | tf_op jit(solution)/shard_map/ppermute | solution.py:581
  11.3 2.4 %collective-permute-start.1 = (f32[144,128]{1,0:T(8,128)}, f32[144,128]{1,0:T(8,128)S(1)}, u32[]{:S(2)}, u32[]{:S(2)}) collective-permute-start(f32[144,128]{1,0:T(8,128)} %get-tuple-element.12), channel_id=1, source_target_pairs={{0,1},{1,0},{2,3},{3,2},{4,5},{5,4},{6,7},{7,6},{8,9},{9,8},{10,11... | collective-permute-start | bytes 221192 | tf_op jit(solution)/shard_map/ppermute | solution.py:582
  13.6 0.6 %copy-start = (f32[144,128]{1,0:T(8,128)}, f32[144,128]{1,0:T(8,128)S(1)}, u32[]{:S(2)}) copy-start(f32[144,128]{1,0:T(8,128)S(1)} %collective-permute-done.far_hbm) | copy-start | bytes 221188
  13.6 0.7 %copy-start.1 = (f32[144,128]{1,0:T(8,128)}, f32[144,128]{1,0:T(8,128)S(1)}, u32[]{:S(2)}) copy-start(f32[144,128]{1,0:T(8,128)S(1)} %collective-permute-done.1.near_hbm) | copy-start | bytes 221188

commit v4 on v3

--- a/solution.py
+++ b/solution.py
@@ -496,7 +496,7 @@
 
 
 WORK = [
-    (2, 1024, 128),
+    (2, 1032, 128),
     (8, 256),
     (2, 128, 128),
     (2, 128, 128),

time: 45.2 us -> 45.2 us (level)
  no operation moved by 1% of the time
where the time goes in v4:
time: 45.2 us; the launch traced here: 44.9 us
  blocking collectives  16.9 us (37%)
  Pallas kernels  15.5 us (34%)
  starting transfers between devices  8.83 us (20%)
  waiting for transfers between devices  2.35 us (5%)
  local copies, waits for them, and re-layouts  0.67 us (1%)
  between operations  0.64 us (1%)
    all_to_all x1, blocking collectives, per_device(): lax.all_to_all(send.reshape(16, 24, 128), 'bead', split_axis=0, concat_ax...  16.9 us
    pallas_call x3, Pallas kernels, call(): pl.pallas_call(kernel, out_shape=[jax.ShapeDtypeStruct(shape, F32) for sh...  15.5 us
    ppermute x1, starting transfers between devices, per_device(): far = lax.ppermute(to_far, 'space', distant)  8.82 us
    ppermute x1, waiting for transfers between devices, per_device(): far = lax.ppermute(to_far, 'space', distant)  2.35 us
  transfers between devices with their start and end apart: 2, of which 1 were waited for; matrix products, arithmetic and copies ran while one was open for 0% of the time, Pallas kernels for 0%

profile of v4, /device:TPU:8, one launch (start us, length us, event | category | flops | bytes accessed | tf_op | source)
XLA Modules:
  0.0 44.9 jit_solution(4531449429921689121)
XLA Ops:
  0.6 1.8 %pack.1 = (f32[16,128]{1,0:T(8,128)}, f32[144,128]{1,0:T(8,128)}, f32[144,128]{1,0:T(8,128)}) custom-call(f32[3,2,256]{2,1,0:T(2,128)} %bitcast.10, s32[1,256]{1,0:T(1,128)} %bitcast.12, s32[2,128]{1,0:T(2,128)} %ghost_ref.1, s32[128,256]{1,0:T(8,128)} %nbr_hbm.1), custom_call_target="tpu_custom_call" | custom-call | tf_op jit(solution)/shard_map/pack/pallas_call | solution.py:556
  2.5 8.8 %collective-permute-start = (f32[144,128]{1,0:T(8,128)}, f32[144,128]{1,0:T(8,128)S(1)}, u32[]{:S(2)}, u32[]{:S(2)}) collective-permute-start(f32[144,128]{1,0:T(8,128)} %get-tuple-element.11), channel_id=1, source_target_pairs={{0,15},{1,2},{2,1},{3,4},{4,3},{5,6},{6,5},{7,8},{8,7},{9,10},{10,... | collective-permute-start | bytes 221192 | tf_op jit(solution)/shard_map/ppermute | solution.py:581
  11.3 0.0 collective-permute-start.1
  11.3 2.3 %collective-permute-done.far_hbm = f32[144,128]{1,0:T(8,128)S(1)} collective-permute-done((f32[144,128]{1,0:T(8,128)}, f32[144,128]{1,0:T(8,128)S(1)}, u32[]{:S(2)}, u32[]{:S(2)}) %collective-permute-start) | collective-permute-done | bytes 73760 | tf_op jit(solution)/shard_map/ppermute | solution.py:581
  13.6 0.0 copy-start
  13.6 0.0 collective-permute-done.1.near_hbm
  13.6 0.0 copy-start.1
  13.6 0.6 %copy-done = f32[144,128]{1,0:T(8,128)} copy-done((f32[144,128]{1,0:T(8,128)}, f32[144,128]{1,0:T(8,128)S(1)}, u32[]{:S(2)}) %copy-start) | copy-done | bytes 73752
  14.3 0.0 copy-done.1
  14.3 13.1 %forces.1 = (f32[3,2,256]{2,1,0:T(2,128)}, f32[384,128]{1,0:T(8,128)}) custom-call(f32[16,128]{1,0:T(8,128)} %get-tuple-element.10.own_hbm, f32[144,128]{1,0:T(8,128)} %copy-done, f32[144,128]{1,0:T(8,128)} %copy-done.1, s32[128,256]{1,0:T(8,128)} %nbr_hbm.1, f32[64,512]{1,0:T(8,128)} %sparse_hbm.1, f32[2,512]{1,0:T(2,128)} %coef_hbm.1, ...), custom_call_target="tpu_custom_call" | custom-call | tf_op jit(solution)/shard_map/forces/pallas_call | solution.py:556
  27.4 16.9 %all_to_all.5.parts_ref = f32[16,24,128]{2,1,0:T(8,128)S(1)} all-to-all(f32[16,24,128]{2,1,0:T(8,128)} %bitcast.8), channel_id=1, replica_groups=mesh['bead'=16,'space'=16] {'bead'}, dimensions={0} | all-to-all | bytes 393216 | tf_op jit(solution)/shard_map/all_to_all | solution.py:593
  44.3 0.6 %finish.1 = (f32[3,2,256]{2,1,0:T(2,128)}, f32[3,2,256]{2,1,0:T(2,128)}) custom-call(f32[16,24,128]{2,1,0:T(8,128)S(1)} %all_to_all.5.parts_ref), custom_call_target="tpu_custom_call" | custom-call | tf_op jit(solution)/shard_map/finish/pallas_call | solution.py:556
Async XLA Ops:
  2.5 11.2 %collective-permute-start = (f32[144,128]{1,0:T(8,128)}, f32[144,128]{1,0:T(8,128)S(1)}, u32[]{:S(2)}, u32[]{:S(2)}) collective-permute-start(f32[144,128]{1,0:T(8,128)} %get-tuple-element.11), channel_id=1, source_target_pairs={{0,15},{1,2},{2,1},{3,4},{4,3},{5,6},{6,5},{7,8},{8,7},{9,10},{10,... | collective-permute-start | bytes 221192 | tf_op jit(solution)/shard_map/ppermute | solution.py:581
  11.3 2.4 %collective-permute-start.1 = (f32[144,128]{1,0:T(8,128)}, f32[144,128]{1,0:T(8,128)S(1)}, u32[]{:S(2)}, u32[]{:S(2)}) collective-permute-start(f32[144,128]{1,0:T(8,128)} %get-tuple-element.12), channel_id=1, source_target_pairs={{0,1},{1,0},{2,3},{3,2},{4,5},{5,4},{6,7},{7,6},{8,9},{9,8},{10,11... | collective-permute-start | bytes 221192 | tf_op jit(solution)/shard_map/ppermute | solution.py:582
  13.6 0.6 %copy-start = (f32[144,128]{1,0:T(8,128)}, f32[144,128]{1,0:T(8,128)S(1)}, u32[]{:S(2)}) copy-start(f32[144,128]{1,0:T(8,128)S(1)} %collective-permute-done.far_hbm) | copy-start | bytes 221188
  13.6 0.7 %copy-start.1 = (f32[144,128]{1,0:T(8,128)}, f32[144,128]{1,0:T(8,128)S(1)}, u32[]{:S(2)}) copy-start(f32[144,128]{1,0:T(8,128)S(1)} %collective-permute-done.1.near_hbm) | copy-start | bytes 221188
